TPU v7x, 512 devices: a whole 4x8x8 slice. The times are simulated.
512 devices in a mesh: segment: 16 (over z, core), seq: 32 (over y, x).
Axes of the slice: x: 4, y: 8, z: 8, core: 2. Of those that a mesh axis runs over, the one named last changes fastest.
Arguments:
- features: bfloat16 [16, 4096, 4096], P('segment', 'seq'), may hold values from -6 to 6
- cotangent: bfloat16 [16, 4096, 4096], P('segment', 'seq'), may hold values from -6 to 6
- short_taps: float32 [16, 3, 3, 4096], P('segment'), may hold values from -3 to 3
- residue: float32 [16, 8, 4096], P('segment'), may hold values from -2 to 2
- decay_rates: float32 [16, 8, 4096], P('segment'), may hold values from 0.00024414062 to 0.05
- lengths: int32 [16, 8], P('segment'), may hold values from 1 to 2048, 4096 in all within a row
Outputs:
- passed: float32 [16, 4096, 4096], P('segment', 'seq')
Inputs may be any that keep to these rules, and one draw needn't show every extreme that they name: Each section's 8 lengths sum to 4096, and the longest is exactly 2048.
All inputs are finite; a program needn't handle non-finite values.
Results may differ from a plain program's by a relative error of at most 0.0004.
Values may be sent and summed in bfloat16 or wider, within the bound.
A program may use at most 128 MiB of HBM per device.

v0:
```python
import jax
import jax.numpy as jnp
from jax import lax
from jax.sharding import PartitionSpec as P

HIGHEST = lax.Precision.HIGHEST


def passed_along(value, axis, by):
    count = lax.axis_size(axis)
    pairs = [(i, i + by) for i in range(count) if 0 <= i + by < count]
    return lax.ppermute(value, axis, pairs)


def entering(part, axis, combine, identity, reverse):
    count = lax.axis_size(axis)
    place = lax.axis_index(axis)
    ahead = count - 1 - place if reverse else place
    gathered = jax.tree.map(lambda a: lax.all_gather(a, axis), part)
    state = jax.tree.map(lambda a, e: jnp.zeros_like(a) + jnp.asarray(e, a.dtype), part, identity)

    def one(lap, state):
        source = count - 1 - lap if reverse else lap
        return combine(
            state, jax.tree.map(lambda a: lax.dynamic_index_in_dim(a, source, 0, False), gathered)
        )

    return lax.fori_loop(0, ahead, one, state)


def passed_along_2(block, axis, distance):
    devices = range(lax.axis_size(axis))
    route = [((i - distance) % len(devices), i) for i in devices]
    return lax.ppermute(block, axis, route)


def compose_full(earlier, later):
    return (earlier[0] * later[0], later[1] + later[0] * earlier[1])


def shards(features, cotangent, short_taps, residue, decay_rates, lengths):
    inputs = features[0]
    grad_out = cotangent[0].astype(jnp.float32)
    tap_table = short_taps[0]
    res_table = residue[0]
    rate_table = decay_rates[0]
    doc_lengths = lengths[0]
    row_count, channels = inputs.shape
    pole_count = rate_table.shape[0]
    seq_devices = lax.axis_size("seq")
    first_row = lax.axis_index("seq") * row_count
    doc_ends = jnp.cumsum(doc_lengths)
    positions = first_row + jnp.arange(-2, row_count + 2, dtype=jnp.int32)
    counted = jnp.sum((doc_ends[None, :] <= positions[:, None]).astype(jnp.int32), axis=1)
    inside = (positions >= 0) & (positions < row_count * seq_devices)
    beside_all = jnp.where(inside, counted, -1)
    doc_ids = beside_all[2 : row_count + 2]
    before = passed_along(inputs[row_count - 2 :], "seq", 1)
    widened = jnp.concatenate([before, inputs], axis=0).astype(jnp.float32)
    streams = []
    for stream in range(3):
        summed = tap_table[stream, 0][None, :] * widened[2:]
        for lag_steps in (1, 2):
            same_doc = (beside_all[2 - lag_steps : row_count + 2 - lag_steps] == doc_ids).astype(
                jnp.float32
            )[:, None]
            summed = (
                summed
                + tap_table[stream, lag_steps][None, :]
                * same_doc
                * widened[2 - lag_steps : row_count + 2 - lag_steps]
            )
        streams.append(summed)
    gate_stream, key_stream, value_stream = streams
    mixed_in = key_stream * value_stream
    grad_filtered = grad_out * gate_stream
    weights = res_table * jnp.sqrt(2.0 * rate_table)
    row_index = jnp.arange(row_count, dtype=jnp.int32)
    row_float = row_index.astype(jnp.float32)
    causal = (
        (row_index[:, None] >= row_index[None, :]) & (doc_ids[:, None] == doc_ids[None, :])
    ).astype(jnp.float32)
    width_block = min(channels, 512)
    block_count = channels // width_block
    flat_shape = (row_count, pole_count * width_block)
    cube_shape = (row_count, pole_count, width_block)

    def first_pass(block_step, partials):
        conv_local, back_local, tail_state, head_state = partials
        offset = block_step * width_block
        rate_part = lax.dynamic_slice_in_dim(rate_table, offset, width_block, 1)
        weight_part = lax.dynamic_slice_in_dim(weights, offset, width_block, 1)
        input_part = lax.dynamic_slice_in_dim(mixed_in, offset, width_block, 1)
        grad_part = lax.dynamic_slice_in_dim(grad_filtered, offset, width_block, 1)
        shrink = jnp.exp(-rate_part[None] * row_float[:, None, None])
        growth = jnp.exp(rate_part[None] * row_float[:, None, None])
        scaled_in = (input_part[:, None, :] * growth).reshape(flat_shape)
        scaled_grad = (grad_part[:, None, :] * shrink).reshape(flat_shape)
        forward = jnp.dot(
            causal, scaled_in, precision=HIGHEST, preferred_element_type=jnp.float32
        ).reshape(cube_shape)
        backward = jnp.dot(
            causal.T, scaled_grad, precision=HIGHEST, preferred_element_type=jnp.float32
        ).reshape(cube_shape)
        held_state = shrink * forward
        conv_local = lax.dynamic_update_slice_in_dim(
            conv_local, jnp.sum(weight_part[None] * held_state, axis=1), offset, 1
        )
        back_local = lax.dynamic_update_slice_in_dim(
            back_local, jnp.sum(weight_part[None] * growth * backward, axis=1), offset, 1
        )
        tail_state = lax.dynamic_update_slice_in_dim(
            tail_state, held_state[row_count - 1], offset, 1
        )
        head_state = lax.dynamic_update_slice_in_dim(head_state, backward[0], offset, 1)
        return (conv_local, back_local, tail_state, head_state)

    zero_rows = jnp.zeros((row_count, channels), jnp.float32)
    zero_state = jnp.zeros((pole_count, channels), jnp.float32)
    conv_local, back_local, tail_state, head_state = lax.fori_loop(
        0, block_count, first_pass, (zero_rows, zero_rows, zero_state, zero_state)
    )
    span_decay = jnp.exp(-rate_table * row_count)
    prev_link = (beside_all[1] == doc_ids[row_count - 1]).astype(jnp.float32)
    next_link = (beside_all[row_count + 2] == doc_ids[0]).astype(jnp.float32)
    identity = (jnp.ones_like(zero_state), zero_state)
    incoming = entering((prev_link * span_decay, tail_state), "seq", compose_full, identity, False)[
        1
    ]
    returned = entering((next_link * span_decay, head_state), "seq", compose_full, identity, True)[
        1
    ]
    enter_mask = (doc_ids == beside_all[1]).astype(jnp.float32)[:, None, None]
    leave_mask = (doc_ids == beside_all[row_count + 2]).astype(jnp.float32)[:, None, None]

    def second_pass(block_step, partials):
        conv_full, back_full = partials
        offset = block_step * width_block
        rate_part = lax.dynamic_slice_in_dim(rate_table, offset, width_block, 1)
        weight_part = lax.dynamic_slice_in_dim(weights, offset, width_block, 1)
        enter_state = lax.dynamic_slice_in_dim(incoming, offset, width_block, 1)
        leave_state = lax.dynamic_slice_in_dim(returned, offset, width_block, 1)
        enter_pow = jnp.exp(-rate_part[None] * (row_float[:, None, None] + 1.0))
        leave_pow = jnp.exp(-rate_part[None] * (row_count - row_float[:, None, None]))
        conv_add = jnp.sum(weight_part[None] * enter_mask * enter_pow * enter_state[None], axis=1)
        back_add = jnp.sum(weight_part[None] * leave_mask * leave_pow * leave_state[None], axis=1)
        conv_full = lax.dynamic_update_slice_in_dim(
            conv_full,
            lax.dynamic_slice_in_dim(conv_full, offset, width_block, 1) + conv_add,
            offset,
            1,
        )
        back_full = lax.dynamic_update_slice_in_dim(
            back_full,
            lax.dynamic_slice_in_dim(back_full, offset, width_block, 1) + back_add,
            offset,
            1,
        )
        return (conv_full, back_full)

    filtered, grad_mixed = lax.fori_loop(0, block_count, second_pass, (conv_local, back_local))
    grad_gate = grad_out * filtered
    grad_key = grad_mixed * value_stream
    grad_value = grad_mixed * key_stream
    grads = (grad_gate, grad_key, grad_value)
    terms = [
        sum((tap_table[stream, lag_steps][None, :] * grads[stream] for stream in range(3)))
        for lag_steps in range(3)
    ]
    after = passed_along(jnp.stack([terms[1][:2], terms[2][:2]]), "seq", -1)
    total = terms[0]
    for lag_steps in (1, 2):
        source = jnp.concatenate([terms[lag_steps], after[lag_steps - 1]], axis=0)
        same_doc = (beside_all[0 + 2 + lag_steps : row_count + 2 + lag_steps] == doc_ids).astype(
            jnp.float32
        )[:, None]
        total = total + same_doc * source[0 + lag_steps : row_count + lag_steps]
    passed = passed_along_2(total, "segment", -1)
    return passed[None]


def solution(mesh):
    in_specs = (
        P("segment", "seq", None),
        P("segment", "seq", None),
        P("segment", None, None, None),
        P("segment", None, None),
        P("segment", None, None),
        P("segment", None),
    )
    out_specs = P("segment", "seq", None)
    return jax.shard_map(shards, mesh=mesh, in_specs=in_specs, out_specs=out_specs, check_vma=False)
```

profile of v0, /device:TPU:59, one launch (start us, length us, event | category | flops | bytes accessed | tf_op | source)
XLA Modules:
  0.0 634.7 jit_solution(1859621096218031744)
XLA Ops:
  21.3 4.0 fusion.39
  28.4 220.6 %while.66 = (s32[]{:T(128)}, f32[128,4096]{1,0:T(8,128)}, f32[128,4096]{1,0:T(8,128)}, f32[8,4096]{1,0:T(8,128)S(1)}, f32[8,4096]{1,0:T(8,128)S(1)}, /*index=5*/...) while((s32[]{:T(128)}, f32[128,4096]{1,0:T(8,128)}, ...), condition=%wide.region_5.6_spmd.clone.clone, body=%wide.region_2.5_spmd.clone.clone.sunk | while | flops 1616912512 | bytes 39193800 | solution.py:120
  32.3 3.6 fusion.59
  40.8 4.9 fusion.60
  48.7 5.3 multiply_reduce_fusion.6
  59.8 3.6 fusion.59
  68.3 4.9 fusion.60
  76.3 5.3 multiply_reduce_fusion.6
  87.4 3.6 fusion.59
  95.9 4.9 fusion.60
  103.8 5.3 multiply_reduce_fusion.6
  115.0 3.6 fusion.59
  123.4 4.9 fusion.60
  131.4 5.3 multiply_reduce_fusion.6
  142.5 3.6 fusion.59
  151.0 4.9 fusion.60
  158.9 5.3 multiply_reduce_fusion.6
  170.1 3.6 fusion.59
  178.5 4.9 fusion.60
  186.5 5.3 multiply_reduce_fusion.6
  206.1 4.9 fusion.60
  214.0 5.3 multiply_reduce_fusion.6
  233.6 4.9 fusion.60
  241.6 5.3 multiply_reduce_fusion.6
  251.1 84.3 %all-gather.13.cloned.1.call-done = f32[256,4096]{1,0:T(8,128)} async-done(((f32[8,4096]{1,0:T(8,128)}), f32[256,4096]{1,0:T(8,128)}) %all-gather.13.cloned.1.call-update) | async-done | bytes 4194320 | tf_op jit(solution)/shard_map/all_gather | solution.py:19
  337.6 85.7 %all-gather.7.cloned.1.call-done = f32[32,8,4096]{2,1,0:T(8,128)} async-done(((f32[1,8,4096]{2,1,0:T(8,128)}), f32[32,8,4096]{2,1,0:T(8,128)}) %all-gather.7.cloned.1.call-update) | async-done | bytes 4194320 | tf_op jit(solution)/shard_map/all_gather | solution.py:19
  423.2 87.7 %all-gather.11.cloned.1.call-done = f32[256,4096]{1,0:T(8,128)} async-done(((f32[8,4096]{1,0:T(8,128)}), f32[256,4096]{1,0:T(8,128)}) %all-gather.11.cloned.1.call-update) | async-done | bytes 4194320 | tf_op jit(solution)/shard_map/all_gather | solution.py:19
  510.9 30.7 %while.64 = (s32[]{:T(128)}, f32[8,4096]{1,0:T(8,128)S(1)}, s32[]{:T(128)}, f32[32,8,4096]{2,1,0:T(8,128)}, f32[32,8,4096]{2,1,0:T(8,128)}, /*index=5*/s32[]{:T(128)}, s32[]{:T(128)}, s32[]{:T(128)}) while((s32[]{:T(128)}, f32[8,4096]{1,0:T(8,128)S(1)}, s32[]{:T(128)}, f32[32,8,4096]{2,1,0:T(8,128)}, f32[32,8,4096]{2,1,0:T(8,128)}, ...), condition=%wide.region_7.8_spmd, body=%wide.region_6.7_spmd.sunk | while | flops 65541 | bytes 524411 | solution.py:28
  541.7 42.9 %while.67 = (s32[]{:T(128)}, f32[128,4096]{1,0:T(8,128)}, f32[128,4096]{1,0:T(8,128)}, f32[8,4096]{1,0:T(8,128)S(1)}, f32[128,1,1]{0,2,1:T(1,128)}, /*index=5*/f...) while((s32[]{:T(128)}, f32[128,4096]{1,0:T(8,128)}, ...), condition=%wide.region_13.14_spmd.clone.clone, body=%wide.region_10.13_spmd.clone.clone.sunk | while | flops 5247494 | bytes 2297023 | solution.py:161
  584.7 4.0 multiply_add_fusion.1
  596.1 5.7 collective-permute-start.2
  601.8 25.0 %collective-permute-done.2 = f32[128,4096]{1,0:T(8,128)S(1)} collective-permute-done((f32[128,4096]{1,0:T(8,128)S(1)}, f32[128,4096]{1,0:T(8,128)S(1)}, u32[]{:S(2)}, u32[]{:S(2)}) %collective-permute-start.2) | collective-permute-done | bytes 2097184 | tf_op jit(solution)/shard_map/ppermute | solution.py:34
  (321 shorter events, 219.9 us)
Async XLA Ops:
  6.5 14.4 %copy-start.6 = (bf16[1,128,4096]{2,1,0:T(8,128)(2,1)S(1)}, bf16[1,128,4096]{2,1,0:T(8,128)(2,1)}, u32[]{:S(2)}) copy-start(bf16[1,128,4096]{2,1,0:T(8,128)(2,1)} %param.14) | copy-start | bytes 3145732
  6.5 244.5 %all-gather.9.cloned.1.call-start = ((), (), s32[]{:S(2)}) async-start(), calls=%async_computation.1 | async-start | bytes 4325376 | tf_op jit(solution)/shard_map/all_gather | solution.py:19
  7.5 13.4 %collective-permute-start = (bf16[2,4096]{1,0:T(2,128)(2,1)S(1)}, bf16[2,4096]{1,0:T(2,128)(2,1)S(1)}, u32[]{:S(2)}, u32[]{:S(2)}) collective-permute-start(bf16[2,4096]{1,0:T(2,128)(2,1)S(1)} %slice_bitcast_fusion.5), channel_id=1, source_target_pairs={{0,1},{1,2},{2,3},{3,4},{4,5},{5,6},{6,7},{7,8},{8,9},{9,10},{10,1... | collective-permute-start | bytes 49160 | tf_op jit(solution)/shard_map/ppermute | solution.py:12
  16.5 318.9 %all-gather.13.cloned.1.call-start = ((), (), s32[]{:S(2)}) async-start(), calls=%async_computation.3 | async-start | bytes 4325376 | tf_op jit(solution)/shard_map/all_gather | solution.py:19
  17.6 3.7 copy-start.4
  17.7 7.5 %copy-start.9 = (f32[1,1,4096]{2,1,0:T(1,128)}, f32[1,1,4096]{2,1,0:T(1,128)S(1)}, u32[]{:S(2)}) copy-start(f32[1,1,4096]{2,1,0:T(1,128)S(1)} %get-tuple-element.688) | copy-start | bytes 49156
  17.7 7.5 %copy-start.11 = (f32[1,1,4096]{2,1,0:T(1,128)}, f32[1,1,4096]{2,1,0:T(1,128)S(1)}, u32[]{:S(2)}) copy-start(f32[1,1,4096]{2,1,0:T(1,128)S(1)} %get-tuple-element.691) | copy-start | bytes 49156
  17.7 7.5 %copy-start.13 = (f32[1,1,4096]{2,1,0:T(1,128)}, f32[1,1,4096]{2,1,0:T(1,128)S(1)}, u32[]{:S(2)}) copy-start(f32[1,1,4096]{2,1,0:T(1,128)S(1)} %get-tuple-element.684) | copy-start | bytes 49156
  17.7 7.5 %copy-start.14 = (f32[1,1,4096]{2,1,0:T(1,128)}, f32[1,1,4096]{2,1,0:T(1,128)S(1)}, u32[]{:S(2)}) copy-start(f32[1,1,4096]{2,1,0:T(1,128)S(1)} %get-tuple-element.685) | copy-start | bytes 49156
  17.7 7.5 %copy-start.15 = (f32[1,1,4096]{2,1,0:T(1,128)}, f32[1,1,4096]{2,1,0:T(1,128)S(1)}, u32[]{:S(2)}) copy-start(f32[1,1,4096]{2,1,0:T(1,128)S(1)} %get-tuple-element.686) | copy-start | bytes 49156
  17.7 7.5 %copy-start.16 = (f32[1,1,4096]{2,1,0:T(1,128)}, f32[1,1,4096]{2,1,0:T(1,128)S(1)}, u32[]{:S(2)}) copy-start(f32[1,1,4096]{2,1,0:T(1,128)S(1)} %get-tuple-element.687) | copy-start | bytes 49156
  17.8 7.5 %copy-start.17 = (f32[1,1,4096]{2,1,0:T(1,128)}, f32[1,1,4096]{2,1,0:T(1,128)S(1)}, u32[]{:S(2)}) copy-start(f32[1,1,4096]{2,1,0:T(1,128)S(1)} %get-tuple-element.689) | copy-start | bytes 49156
  17.8 7.5 %copy-start.18 = (f32[1,1,4096]{2,1,0:T(1,128)}, f32[1,1,4096]{2,1,0:T(1,128)S(1)}, u32[]{:S(2)}) copy-start(f32[1,1,4096]{2,1,0:T(1,128)S(1)} %get-tuple-element.690) | copy-start | bytes 49156
  249.1 0.7 copy-start.8
  249.1 1.5 copy-start.7
  249.7 173.5 %all-gather.7.cloned.1.call-start = ((), (), s32[]{:S(2)}) async-start(), calls=%async_computation | async-start | bytes 4325376 | tf_op jit(solution)/shard_map/all_gather | solution.py:19
  250.5 260.4 %all-gather.11.cloned.1.call-start = ((), (), s32[]{:S(2)}) async-start(), calls=%async_computation.2 | async-start | bytes 4325376 | tf_op jit(solution)/shard_map/all_gather | solution.py:19
  541.7 42.9 %copy-start.2 = (f32[128,4096]{1,0:T(8,128)S(1)}, f32[128,4096]{1,0:T(8,128)}, u32[]{:S(2)}) copy-start(f32[128,4096]{1,0:T(8,128)} %get-tuple-element.672) | copy-start | bytes 6291460
  541.7 42.9 %copy-start.5 = (bf16[1,128,4096]{2,1,0:T(8,128)(2,1)S(1)}, bf16[1,128,4096]{2,1,0:T(8,128)(2,1)}, u32[]{:S(2)}) copy-start(bf16[1,128,4096]{2,1,0:T(8,128)(2,1)} %param.15) | copy-start | bytes 3145732
  584.6 9.7 %copy-start = (f32[128,4096]{1,0:T(8,128)S(1)}, f32[128,4096]{1,0:T(8,128)}, u32[]{:S(2)}) copy-start(f32[128,4096]{1,0:T(8,128)} %get-tuple-element.508) | copy-start | bytes 6291460
  584.6 9.7 %copy-start.1 = (f32[128,4096]{1,0:T(8,128)S(1)}, f32[128,4096]{1,0:T(8,128)}, u32[]{:S(2)}) copy-start(f32[128,4096]{1,0:T(8,128)} %get-tuple-element.509) | copy-start | bytes 6291460
  584.6 9.7 %copy-start.3 = (f32[128,4096]{1,0:T(8,128)S(1)}, f32[128,4096]{1,0:T(8,128)}, u32[]{:S(2)}) copy-start(f32[128,4096]{1,0:T(8,128)} %get-tuple-element.673) | copy-start | bytes 6291460
  584.6 9.7 %copy-start.10 = (f32[1,1,4096]{2,1,0:T(1,128)S(1)}, f32[1,1,4096]{2,1,0:T(1,128)}, u32[]{:S(2)}) copy-start(f32[1,1,4096]{2,1,0:T(1,128)} %copy-done.9) | copy-start | bytes 49156
  584.7 9.7 %copy-start.12 = (f32[1,1,4096]{2,1,0:T(1,128)S(1)}, f32[1,1,4096]{2,1,0:T(1,128)}, u32[]{:S(2)}) copy-start(f32[1,1,4096]{2,1,0:T(1,128)} %copy-done.11) | copy-start | bytes 49156
  584.7 9.7 %copy-start.19 = (f32[128]{0:T(128)S(1)}, f32[128]{0:T(128)}, u32[]{:S(2)}) copy-start(f32[128]{0:T(128)} %get-tuple-element.696) | copy-start | bytes 1540
  584.7 9.7 %copy-start.20 = (f32[128]{0:T(128)S(1)}, f32[128]{0:T(128)}, u32[]{:S(2)}) copy-start(f32[128]{0:T(128)} %get-tuple-element.699) | copy-start | bytes 1540
  588.8 5.5 collective-permute-start.1
  596.1 30.7 %collective-permute-start.2 = (f32[128,4096]{1,0:T(8,128)S(1)}, f32[128,4096]{1,0:T(8,128)S(1)}, u32[]{:S(2)}, u32[]{:S(2)}) collective-permute-start(f32[128,4096]{1,0:T(8,128)S(1)} %fusion.31), channel_id=1, source_target_pairs={{32,0},{64,32},{96,64},{128,96},{160,128},{192,160},{224,192},{256... | collective-permute-start | bytes 6291464 | tf_op jit(solution)/shard_map/ppermute | solution.py:34
Sparse Core Ops, SparseCore 0:
  16.6 85.3 all-gather.8
  249.9 85.4 all-gather.12
  338.6 84.6 all-gather.6
  426.3 84.6 all-gather.10
where the time goes:
time: 638 us; the launch traced here: 635 us
  waiting for transfers between devices  286 us (45%)
  other arithmetic  139 us (22%)
  local copies, waits for them, and re-layouts  112 us (18%)
  matrix products  67.4 us (11%)
  between operations  16.1 us (3%)
  starting transfers between devices  11.9 us (2%)
    all_gather x4, waiting for transfers between devices, entering(): gathered = jax.tree.map(lambda a: lax.all_gather(a, axis), part)  258 us
    reduce_sum x8, other arithmetic, first_pass(): jnp.sum(weight_part[None] * growth * backward, axis=1)  42.5 us
    dot_general x8, matrix products, first_pass(): jnp.dot(causal, scaled_in, precision=HIGHEST, preferred_element_type=jnp....  39 us
    add x31, other arithmetic, compose_full(): return (earlier[0] * later[0], later[1] + later[0] * earlier[1])  32.1 us
    dot_general x8, matrix products, first_pass(): jnp.dot(causal.T, scaled_grad, precision=HIGHEST, preferred_element_type=...  28.5 us
    while x32, local copies, waits for them, and re-layouts  26.3 us
    ppermute x1, waiting for transfers between devices, passed_along_2(): return lax.ppermute(block, axis, route)  25 us
    reshape x8, local copies, waits for them, and re-layouts, first_pass(): forward = jnp.dot(causal, scaled_in, precision=HIGHEST, preferred_element...  24.5 us
  transfers between devices with their start and end apart: 7, of which 5 were waited for; matrix products, arithmetic and copies ran while one was open for 37% of the time, Pallas kernels for 0%

commit v1 on v0

v1 whole, which is shorter than its diff:
```python
import jax
import jax.numpy as jnp
from jax import lax
from jax.experimental import pallas as pl
from jax.experimental.pallas import tpu as pltpu
from jax.sharding import PartitionSpec as P

MESH = pl.DeviceIdType.MESH
F32 = jnp.float32
TOK = 128
HALO = 2
LANES = 128
GROUP = 8
WIDTH = GROUP * LANES
PARTS = 4
POLES = 8
DOCS = 8
ROWS = 8
XS = TOK + 2 * HALO
ES = TOK + HALO
STATE = POLES * GROUP
TOP = 32767.0


def tile(ref, i):
    return ref[pl.ds(pl.multiple_of(i * GROUP, GROUP), GROUP), :]


def put(ref, i, value):
    ref[pl.ds(pl.multiple_of(i * GROUP, GROUP), GROUP), :] = value


def total_of(values):
    values = list(values)
    while len(values) > 1:
        values = [a + b for a, b in zip(values[::2], values[1::2])] + (
            [values[-1]] if len(values) % 2 else []
        )
    return values[0]


def mixer_kernel(
    feat, cot, taps, res, rates, lens, out_q, out_s,
    feat_v, cot_v, taps_v, res_v, rates_v,
    xt, gt, kt, vt, gft, ft, ot, k1, k2, mt, mh,
    tap_t, dec, wts, dd, dd4,
    tails, row_in, sums, col_in, sent, inc, qv, sv, iv,
    load_sem, par_sem, halo_send, halo_recv, tail_send, tail_recv,
    col_send, col_recv, inc_send, inc_recv, out_send, out_recv,
):
    sg = lax.axis_index("segment")
    q = lax.axis_index("seq")
    n_sg = lax.axis_size("segment")
    n_q = lax.axis_size("seq")
    y, x = q // PARTS, q % PARTS
    before, after = (q + n_q - 1) % n_q, (q + 1) % n_q
    sg_to, sg_from = (sg + n_sg - 1) % n_sg, (sg + 1) % n_sg

    def row_mate(k):
        return y * PARTS + (x + k) % PARTS

    def col_mate(k):
        return ((y + k) % ROWS) * PARTS + x

    loads = []
    for c in range(PARTS):
        cols = pl.ds(c * WIDTH, WIDTH)
        loads.append((
            pltpu.make_async_copy(feat.at[0, :, cols], feat_v.at[c], load_sem.at[0, c]),
            pltpu.make_async_copy(cot.at[0, :, cols], cot_v.at[c], load_sem.at[1, c]),
        ))
    pars = [
        pltpu.make_async_copy(taps.at[0], taps_v, par_sem.at[0]),
        pltpu.make_async_copy(res.at[0], res_v, par_sem.at[1]),
        pltpu.make_async_copy(rates.at[0], rates_v, par_sem.at[2]),
    ]
    for copy in loads[0]:
        copy.start()
    for copy in pars:
        copy.start()
    for pair in loads[1:]:
        for copy in pair:
            copy.start()

    barrier = pltpu.get_barrier_semaphore()

    def greet(**where):
        pl.semaphore_signal(barrier, inc=1, device_id=where, device_id_type=MESH)

    for k in range(1, PARTS):
        greet(seq=row_mate(k))
    for k in range(1, ROWS):
        greet(seq=col_mate(k))
    greet(seq=before)
    greet(seq=after)
    greet(segment=sg_to)
    greet(segment=sg_from)

    ends = []
    run = jnp.int32(0)
    for i in range(DOCS):
        run = run + lens[0, i]
        ends.append(jnp.full((GROUP, LANES), run, jnp.int32))

    def doc_at(position):
        spot = jnp.full((GROUP, LANES), position, jnp.int32)
        count = total_of([jnp.where(end <= spot, 1, 0) for end in ends])
        return jnp.where(spot < 0, -1, count)

    def same(a, b):
        return jnp.where(a == b, 1.0, 0.0).astype(F32)

    first = q * TOK
    doc_tail = doc_at(first + TOK - 1)
    doc_head = doc_at(first + HALO)

    def mask_step(e, carry):
        d1, d2 = carry
        d0 = doc_at(first + e)
        put(k1, e, same(d0, d1))
        put(k2, e, same(d0, d2))
        put(mt, e, same(d0, doc_tail))
        put(mh, e, same(d0, doc_head))
        return d0, d1

    lax.fori_loop(0, XS, mask_step, (doc_at(first - 1), doc_at(first - 2)))

    for copy in pars:
        copy.wait()
    for c in range(PARTS):
        for g in range(GROUP):
            cols = slice(c * WIDTH + g * LANES, c * WIDTH + (g + 1) * LANES)
            rate = rates_v[:, cols]
            spread = pl.ds(c * STATE + g, POLES, stride=GROUP)
            dec[spread, :] = jnp.exp(-rate)
            dd[spread, :] = jnp.exp(-rate * float(TOK))
            dd4[spread, :] = jnp.exp(-rate * float(TOK * PARTS))
            wts[spread, :] = res_v[:, cols] * jnp.sqrt(2.0 * rate)
            for stream in range(3):
                for lag in range(3):
                    row = (c * 9 + stream * 3 + lag) * GROUP + g
                    tap_t[row : row + 1, :] = taps_v[stream, lag : lag + 1, cols]

    def relay(c, _):
        for which, (source, target, slots, shift) in enumerate(
            ((feat_v, xt, XS, HALO), (cot_v, gt, ES, 0))
        ):
            pltpu.make_async_copy(
                (feat, cot)[which].at[0, :, pl.ds(0, WIDTH)], source.at[c], load_sem.at[which, c]
            ).wait()

            def rows(t, _):
                for g in range(GROUP):
                    value = source[
                        c, pl.ds(pl.multiple_of(t * 16, 16), 16), g * LANES : (g + 1) * LANES
                    ].astype(F32)
                    target[
                        pl.ds((c * slots + shift + t * 16) * GROUP + g, 16, stride=GROUP), :
                    ] = value
                return 0

            lax.fori_loop(0, TOK // 16, rows, 0)
        return 0

    def halo_copies(c):
        def spot(ref, slots, at):
            return ref.at[pl.ds(pl.multiple_of((c * slots + at) * GROUP, GROUP), HALO * GROUP), :]

        return [
            pltpu.make_async_remote_copy(
                src_ref=spot(ref, slots, here),
                dst_ref=spot(ref, slots, there),
                send_sem=halo_send.at[c, n],
                recv_sem=halo_recv.at[c, n],
                device_id={"seq": to},
                device_id_type=MESH,
            )
            for n, (ref, slots, here, there, to) in enumerate((
                (xt, XS, TOK, 0, after),
                (xt, XS, HALO, TOK + HALO, before),
                (gt, ES, 0, TOK, before),
            ))
        ]

    lax.fori_loop(0, 1, relay, 0)
    pl.semaphore_wait(barrier, (PARTS - 1) + (ROWS - 1) + 4)

    def send_halo(c, _):
        for copy in halo_copies(c):
            copy.start()
        return 0

    send_halo(0, 0)

    def relay_and_send(c, _):
        relay(c, 0)
        send_halo(c, 0)
        return 0

    lax.fori_loop(1, PARTS, relay_and_send, 0)

    def tail_copy(c):
        return pltpu.make_async_remote_copy(
            src_ref=tails.at[pl.ds(pl.multiple_of(c * 2 * STATE, 8), 2 * STATE), :],
            dst_ref=row_in.at[pl.ds(pl.multiple_of(x * 2 * STATE, 8), 2 * STATE), :],
            send_sem=tail_send.at[c],
            recv_sem=tail_recv.at[x],
            device_id={"seq": y * PARTS + c},
            device_id_type=MESH,
        )

    def first_pass(c, _):
        for copy in halo_copies(c):
            copy.wait_recv()
        tap = [tile(tap_t, c * 9 + n) for n in range(9)]
        x_at, e_at = c * XS, c * ES

        def streams(i, carry):
            x1, x2 = carry
            for u in range(5):
                e = i * 5 + u
                x0 = tile(xt, x_at + HALO + e)
                a, b = x1 * tile(k1, e), x2 * tile(k2, e)
                gate, key, value = (
                    tap[3 * n] * x0 + tap[3 * n + 1] * a + tap[3 * n + 2] * b for n in range(3)
                )
                put(kt, e_at + e, key)
                put(vt, e_at + e, value)
                put(gft, e_at + e, tile(gt, e_at + e) * gate)
                x1, x2 = x0, x1
            return x1, x2

        lax.fori_loop(0, ES // 5, streams, (tile(xt, x_at + 1), tile(xt, x_at)))

        decay = [tile(dec, c * POLES + p) for p in range(POLES)]

        def ends_step(i, carry):
            fwd, bwd = carry
            for u in range(4):
                e = i * 4 + u
                r = ES - 1 - e
                mixed = tile(kt, e_at + e) * tile(vt, e_at + e) * tile(mt, e)
                grad = tile(gft, e_at + r) * tile(mh, r)
                fwd = tuple(d * s + mixed for d, s in zip(decay, fwd))
                bwd = tuple(d * s + grad for d, s in zip(decay, bwd))
            return fwd, bwd

        zero = tuple(jnp.zeros((GROUP, LANES), F32) for _ in range(POLES))
        fwd, bwd = lax.fori_loop(0, TOK // 4, ends_step, (zero, zero))
        for p in range(POLES):
            put(tails, c * 2 * POLES + p, fwd[p])
            put(tails, c * 2 * POLES + POLES + p, bwd[p])

        @pl.when(c != x)
        def _():
            tail_copy(c).start()

        @pl.when(c == x)
        def _():
            for p in range(2 * POLES):
                put(row_in, x * 2 * POLES + p, tile(tails, c * 2 * POLES + p))

        return 0

    lax.fori_loop(0, PARTS, first_pass, 0)

    for k in range(1, PARTS):
        other = (x + k) % PARTS
        pltpu.make_async_remote_copy(
            src_ref=tails.at[pl.ds(0, 2 * STATE), :],
            dst_ref=row_in.at[pl.ds(pl.multiple_of(other * 2 * STATE, 8), 2 * STATE), :],
            send_sem=tail_send.at[other],
            recv_sem=tail_recv.at[other],
            device_id={"seq": row_mate(k)},
            device_id_type=MESH,
        ).wait_recv()

    row_first = y * PARTS * TOK
    fwd_docs = [doc_at(row_first + n * TOK - 1) for n in range(PARTS + 1)]
    bwd_docs = [doc_at(row_first + n * TOK + HALO) for n in range(PARTS + 1)]
    fwd_link = [same(fwd_docs[n], fwd_docs[n + 1]) for n in range(PARTS)]
    bwd_link = [same(bwd_docs[n], bwd_docs[n + 1]) for n in range(PARTS)]

    def row_total(p, _):
        span = tile(dd, x * POLES + p)
        forward = tile(row_in, p)
        for n in range(1, PARTS):
            forward = tile(row_in, n * 2 * POLES + p) + fwd_link[n] * span * forward
        put(sums, p, forward)
        backward = tile(row_in, (PARTS - 1) * 2 * POLES + POLES + p)
        for n in range(PARTS - 2, -1, -1):
            backward = tile(row_in, n * 2 * POLES + POLES + p) + bwd_link[n] * span * backward
        put(sums, POLES + p, backward)
        return 0

    lax.fori_loop(0, POLES, row_total, 0)

    def col_copy(way, k):
        slot = way * PARTS + k - 1
        return pltpu.make_async_remote_copy(
            src_ref=sums.at[pl.ds(way * STATE, STATE), :],
            dst_ref=col_in.at[pl.ds(slot * STATE, STATE), :],
            send_sem=col_send.at[slot],
            recv_sem=col_recv.at[slot],
            device_id={"seq": col_mate(k if way == 0 else ROWS - k)},
            device_id_type=MESH,
        )

    reach = 4
    for k in range(1, reach + 1):
        for way in range(2):
            col_copy(way, k).start()

    row_span = TOK * PARTS
    past = [doc_at(row_first - k * row_span - 1) for k in range(0, reach)]
    coming = [doc_at(row_first + k * row_span + HALO) for k in range(1, reach + 1)]
    past_link = [same(past[n], past[n + 1]) for n in range(reach - 1)]
    coming_link = [same(coming[n], coming[n + 1]) for n in range(reach - 1)]

    for k in range(1, reach + 1):
        for way in range(2):
            col_copy(way, k).wait_recv()

    def entering(p, _):
        span, long_span = tile(dd, x * POLES + p), tile(dd4, x * POLES + p)
        for way, links in ((0, past_link), (1, coming_link)):
            state = tile(col_in, (way * PARTS + reach - 1) * POLES + p)
            for k in range(reach - 1, 0, -1):
                state = (
                    tile(col_in, (way * PARTS + k - 1) * POLES + p)
                    + links[k - 1] * long_span * state
                )
            order = range(PARTS) if way == 0 else range(PARTS - 1, -1, -1)
            for n in order:
                put(sent, n * 2 * POLES + way * POLES + p, state)
                link = fwd_link[n] if way == 0 else bwd_link[n]
                own = tile(row_in, n * 2 * POLES + way * POLES + p)
                state = own + link * span * state
        return 0

    lax.fori_loop(0, POLES, entering, 0)

    def inc_copy(k):
        other = (x + k) % PARTS
        return pltpu.make_async_remote_copy(
            src_ref=sent.at[pl.ds(pl.multiple_of(other * 2 * STATE, 8), 2 * STATE), :],
            dst_ref=inc.at[pl.ds(pl.multiple_of(x * 2 * STATE, 8), 2 * STATE), :],
            send_sem=inc_send.at[other],
            recv_sem=inc_recv.at[x],
            device_id={"seq": row_mate(k)},
            device_id_type=MESH,
        )

    for k in range(1, PARTS):
        inc_copy(k).start()
    for p in range(2 * POLES):
        put(inc, x * 2 * POLES + p, tile(sent, x * 2 * POLES + p))

    def out_copies(c):
        cols = pl.ds(pl.multiple_of(c * WIDTH, WIDTH), WIDTH)
        scale_rows = pl.ds(pl.multiple_of(c * GROUP, GROUP), GROUP)
        return [
            pltpu.make_async_remote_copy(
                src_ref=source,
                dst_ref=target,
                send_sem=out_send.at[n, c],
                recv_sem=out_recv.at[n, c],
                device_id={"segment": sg_to},
                device_id_type=MESH,
            )
            for n, (source, target) in enumerate((
                (qv.at[c], out_q.at[:, cols]),
                (sv.at[scale_rows, :], out_s.at[scale_rows, :]),
            ))
        ]

    def second_pass(step, _):
        c = (x + step) % PARTS

        @pl.when(step > 0)
        def _():
            pltpu.make_async_remote_copy(
                src_ref=sent.at[pl.ds(0, 2 * STATE), :],
                dst_ref=inc.at[pl.ds(pl.multiple_of(c * 2 * STATE, 8), 2 * STATE), :],
                send_sem=inc_send.at[c],
                recv_sem=inc_recv.at[c],
                device_id={"seq": y * PARTS + c},
                device_id_type=MESH,
            ).wait_recv()

        e_at = c * ES
        decay = [tile(dec, c * POLES + p) for p in range(POLES)]
        weight = [tile(wts, c * POLES + p) for p in range(POLES)]

        def forward(i, state):
            for u in range(5):
                e = i * 5 + u
                mixed = tile(kt, e_at + e) * tile(vt, e_at + e)
                keep = tile(k1, e)
                state = tuple((keep * d) * s + mixed for d, s in zip(decay, state))
                filtered = total_of([w * s for w, s in zip(weight, state)])
                put(ft, e, filtered * tile(gt, e_at + e))
            return state

        lax.fori_loop(
            0, ES // 5, forward, tuple(tile(inc, c * 2 * POLES + p) for p in range(POLES))
        )
        tap = [tile(tap_t, c * 9 + n) for n in range(9)]

        def back_step(e, carry):
            state, t1, t2, t22, most = carry
            grad = tile(gft, e_at + e)
            keep, skip = tile(k1, e + 1), tile(k2, e + 2)
            state = tuple((keep * d) * s + grad for d, s in zip(decay, state))
            mixed = total_of([w * s for w, s in zip(weight, state)])
            grads = (tile(ft, e), mixed * tile(vt, e_at + e), mixed * tile(kt, e_at + e))
            terms = [
                tap[lag] * grads[0] + tap[3 + lag] * grads[1] + tap[6 + lag] * grads[2]
                for lag in range(3)
            ]
            result = terms[0] + keep * t1 + skip * t22
            return result, (state, terms[1], terms[2], t2, most)

        nothing = jnp.zeros((GROUP, LANES), F32)
        carry = (
            tuple(tile(inc, c * 2 * POLES + POLES + p) for p in range(POLES)),
            nothing, nothing, nothing, nothing,
        )
        for e in (TOK + 1, TOK):
            _, carry = back_step(e, carry)

        def backward(i, carry):
            for u in range(4):
                e = TOK - 1 - (i * 4 + u)
                result, (state, t1, t2, t22, most) = back_step(e, carry)
                put(ot, e, result)
                carry = (state, t1, t2, t22, jnp.maximum(most, jnp.abs(result)))
            return carry

        carry = lax.fori_loop(0, TOK // 4, backward, carry)
        most = jnp.maximum(carry[4], 1e-30)
        put(sv, c, most * (1.0 / TOP))
        iv[...] = TOP / most

        def coded(t, _):
            for g in range(GROUP):
                value = ot[pl.ds(t * 16 * GROUP + g, 16, stride=GROUP), :] * iv[g : g + 1, :]
                qv[c, pl.ds(pl.multiple_of(t * 16, 16), 16), g * LANES : (g + 1) * LANES] = (
                    jnp.round(value).astype(jnp.int32).astype(jnp.int16)
                )
            return 0

        lax.fori_loop(0, TOK // 16, coded, 0)
        for copy in out_copies(c):
            copy.start()
        return 0

    lax.fori_loop(0, PARTS, second_pass, 0)

    def finish(c, _):
        for copy in halo_copies(c):
            copy.wait_send()

        @pl.when(c != x)
        def _():
            tail_copy(c).wait_send()

        for copy in out_copies(c):
            copy.wait()
        return 0

    lax.fori_loop(0, PARTS, finish, 0)
    for k in range(1, reach + 1):
        for way in range(2):
            col_copy(way, k).wait_send()
    for k in range(1, PARTS):
        inc_copy(k).wait_send()


def shards(features, cotangent, short_taps, residue, decay_rates, lengths):
    tokens, channels = features.shape[1:]
    any_space = pl.BlockSpec(memory_space=pl.ANY)
    bf16 = jnp.bfloat16
    vm = pltpu.VMEM
    dma = pltpu.SemaphoreType.DMA
    whole = lambda rows: vm((rows * GROUP, LANES), F32)
    coded, scale = pl.pallas_call(
        mixer_kernel,
        out_shape=(
            jax.ShapeDtypeStruct((tokens, channels), jnp.int16),
            jax.ShapeDtypeStruct((PARTS * GROUP, LANES), F32),
        ),
        in_specs=[any_space] * 5 + [pl.BlockSpec(memory_space=pltpu.SMEM)],
        out_specs=(any_space, any_space),
        scratch_shapes=[
            vm((PARTS, TOK, WIDTH), bf16), vm((PARTS, TOK, WIDTH), bf16),
            vm((3, 3, channels), F32), vm((POLES, channels), F32), vm((POLES, channels), F32),
            whole(PARTS * XS), whole(PARTS * ES), whole(PARTS * ES), whole(PARTS * ES),
            whole(PARTS * ES), whole(ES), whole(ES),
            whole(XS), whole(XS), whole(XS), whole(XS),
            whole(PARTS * 9), whole(PARTS * POLES), whole(PARTS * POLES),
            whole(PARTS * POLES), whole(PARTS * POLES),
            whole(PARTS * 2 * POLES), whole(PARTS * 2 * POLES), whole(2 * POLES),
            whole(2 * PARTS * POLES), whole(PARTS * 2 * POLES), whole(PARTS * 2 * POLES),
            vm((PARTS, TOK, WIDTH), jnp.int16), whole(PARTS), whole(1),
            dma((2, PARTS)), dma((3,)), dma((PARTS, 3)), dma((PARTS, 3)),
            dma((PARTS,)), dma((PARTS,)), dma((2 * PARTS,)), dma((2 * PARTS,)),
            dma((PARTS,)), dma((PARTS,)), dma((2, PARTS)), dma((2, PARTS)),
        ],
        compiler_params=pltpu.CompilerParams(
            collective_id=0, has_side_effects=True, vmem_limit_bytes=40 * 1024 * 1024
        ),
        cost_estimate=pl.CostEstimate(
            flops=160 * tokens * channels, bytes_accessed=8 * tokens * channels, transcendentals=0
        ),
    )(features, cotangent, short_taps, residue, decay_rates, lengths)
    return (coded.astype(F32) * scale.reshape(1, channels))[None]


def solution(mesh):
    in_specs = (
        P("segment", "seq", None),
        P("segment", "seq", None),
        P("segment", None, None, None),
        P("segment", None, None),
        P("segment", None, None),
        P("segment", None),
    )
    out_specs = P("segment", "seq", None)
    return jax.shard_map(shards, mesh=mesh, in_specs=in_specs, out_specs=out_specs, check_vma=False)
```

time: 638 us -> 60.3 us (0.09)
  the two profiles are of different devices: /device:TPU:59 before, /device:TPU:4 now
where the time goes in v1:
time: 60.3 us; the launch traced here: 60 us
  Pallas kernels  52.4 us (87%)
  local copies, waits for them, and re-layouts  5.92 us (10%)
  other arithmetic  1.69 us (3%)
    pallas_call x1, Pallas kernels, shards(): pl.pallas_call(mixer_kernel, out_shape=(jax.ShapeDtypeStruct((tokens, cha...  52.4 us
    unnamed x11, local copies, waits for them, and re-layouts  5.92 us
    broadcast_in_dim x1, other arithmetic, shards(): return (coded.astype(F32) * scale.reshape(1, channels))[None]  1.69 us

profile of v1, /device:TPU:4, one launch (start us, length us, event | category | flops | bytes accessed | tf_op | source)
XLA Modules:
  0.0 60.0 jit_solution(1937652573729099296)
XLA Ops:
  0.0 1.0 %copy.7.taps = f32[1,3,3,4096]{3,2,1,0:T(4,128)S(1)} copy(f32[1,3,3,4096]{3,0,2,1:T(1,128)} %param.8) | data formatting | bytes 294912 | tf_op args[2]
  1.0 0.0 copy-start
  1.0 1.2 %copy-done = bf16[1,128,4096]{2,1,0:T(8,128)(2,1)S(1)} copy-done((bf16[1,128,4096]{2,1,0:T(8,128)(2,1)S(1)}, bf16[1,128,4096]{2,1,0:T(8,128)(2,1)}, u32[]{:S(2)}) %copy-start) | copy-done | bytes 1048600
  2.2 0.0 copy-start.1
  2.2 1.2 %copy-done.1 = bf16[1,128,4096]{2,1,0:T(8,128)(2,1)S(1)} copy-done((bf16[1,128,4096]{2,1,0:T(8,128)(2,1)S(1)}, bf16[1,128,4096]{2,1,0:T(8,128)(2,1)}, u32[]{:S(2)}) %copy-start.1) | copy-done | bytes 1048600
  3.5 0.0 copy-start.2
  3.5 0.9 %copy-done.2 = f32[1,8,4096]{2,1,0:T(8,128)S(1)} copy-done((f32[1,8,4096]{2,1,0:T(8,128)S(1)}, f32[1,8,4096]{2,1,0:T(8,128)}, u32[]{:S(2)}) %copy-start.2) | copy-done | bytes 131096
  4.4 0.0 copy-start.3
  4.4 0.9 %copy-done.3 = f32[1,8,4096]{2,1,0:T(8,128)S(1)} copy-done((f32[1,8,4096]{2,1,0:T(8,128)S(1)}, f32[1,8,4096]{2,1,0:T(8,128)}, u32[]{:S(2)}) %copy-start.3) | copy-done | bytes 131096
  5.3 0.0 copy-start.4
  5.3 0.7 %copy-done.4 = s32[1,8]{1,0:T(1,128)S(1)} copy-done((s32[1,8]{1,0:T(1,128)S(1)}, s32[1,8]{1,0:T(1,128)}, u32[]{:S(2)}) %copy-start.4) | copy-done | bytes 56
  5.9 52.4 %shard_map.64 = (s16[128,4096]{1,0:T(8,128)(2,1)S(1)}, f32[32,128]{1,0:T(8,128)S(1)}) custom-call(bf16[1,128,4096]{2,1,0:T(8,128)(2,1)S(1)} %copy-done, bf16[1,128,4096]{2,1,0:T(8,128)(2,1)S(1)} %copy-done.1, f32[1,3,3,4096]{3,2,1,0:T(4,128)S(1)} %copy.7.taps, f32[1,8,4096]{2,1,0:T(8,128)S(1)} %copy-done.2, f32[1,8,4096]{2,1,0:T(8,128)S(1)} %copy-done.3, ...), custom_call_target="tpu_custom_call" | custom-call | flops 83886080 | bytes 4194304 | tf_op jit(solution)/shard_map/pallas_call | solution.py:487
  58.3 1.7 %multiply_bitcast_fusion = f32[1,128,4096]{2,1,0:T(8,128)} fusion(s16[128,4096]{1,0:T(8,128)(2,1)S(1)} %get-tuple-element.7, f32[4096]{0:T(1024)S(1)} %bitcast.3), kind=kLoop, calls=%fused_computation | loop fusion | flops 1048576 | bytes 3162112 | tf_op jit(solution)/shard_map/broadcast_in_dim | solution.py:517
Async XLA Ops:
  1.0 1.2 %copy-start = (bf16[1,128,4096]{2,1,0:T(8,128)(2,1)S(1)}, bf16[1,128,4096]{2,1,0:T(8,128)(2,1)}, u32[]{:S(2)}) copy-start(bf16[1,128,4096]{2,1,0:T(8,128)(2,1)} %feat.1) | copy-start | bytes 3145732
  2.2 1.2 %copy-start.1 = (bf16[1,128,4096]{2,1,0:T(8,128)(2,1)S(1)}, bf16[1,128,4096]{2,1,0:T(8,128)(2,1)}, u32[]{:S(2)}) copy-start(bf16[1,128,4096]{2,1,0:T(8,128)(2,1)} %cot.1) | copy-start | bytes 3145732
  3.5 0.9 %copy-start.2 = (f32[1,8,4096]{2,1,0:T(8,128)S(1)}, f32[1,8,4096]{2,1,0:T(8,128)}, u32[]{:S(2)}) copy-start(f32[1,8,4096]{2,1,0:T(8,128)} %res.1) | copy-start | bytes 393220
  4.4 0.9 %copy-start.3 = (f32[1,8,4096]{2,1,0:T(8,128)S(1)}, f32[1,8,4096]{2,1,0:T(8,128)}, u32[]{:S(2)}) copy-start(f32[1,8,4096]{2,1,0:T(8,128)} %rates.1) | copy-start | bytes 393220
  5.3 0.7 %copy-start.4 = (s32[1,8]{1,0:T(1,128)S(1)}, s32[1,8]{1,0:T(1,128)}, u32[]{:S(2)}) copy-start(s32[1,8]{1,0:T(1,128)} %lens.1) | copy-start | bytes 100

commit v2 on v1

v2 whole, which is shorter than its diff:
```python
import jax
import jax.numpy as jnp
from jax import lax
from jax.experimental import pallas as pl
from jax.experimental.pallas import tpu as pltpu
from jax.sharding import PartitionSpec as P

MESH = pl.DeviceIdType.MESH
F32 = jnp.float32
TOK = 128
HALO = 2
LANES = 128
GROUP = 8
WIDTH = GROUP * LANES
PARTS = 4
POLES = 8
DOCS = 8
ROWS = 8
REACH = 4
XS = TOK + 2 * HALO
ES = TOK + HALO
HALF = TOK // 2
STATE = POLES * GROUP
PAIR = POLES // PARTS
CELL = 2 * PAIR
TOP = 32767.0


def tile(ref, i):
    return ref[pl.ds(pl.multiple_of(i * GROUP, GROUP), GROUP), :]


def put(ref, i, value):
    ref[pl.ds(pl.multiple_of(i * GROUP, GROUP), GROUP), :] = value


def total_of(values):
    values = list(values)
    while len(values) > 1:
        values = [a + b for a, b in zip(values[::2], values[1::2])] + (
            [values[-1]] if len(values) % 2 else []
        )
    return values[0]


def mixer_kernel(
    feat, cot, taps, res, rates, lens, out_q, out_late, out_early,
    feat_v, cot_v, feat_e, cot_e, res_v, rates_v,
    xt, gt, kt, vt, gft, ft, mx, ot, k1, k2, mt, mh, mi, mo,
    tap_t, dec, wts, near, past, grow, dd, dd4,
    tails, row_in, sums, col_in, sent, inc, row_link, col_link, qv, sv, iv,
    load_sem, par_sem, halo_send, halo_recv, tail_send, tail_recv,
    col_send, col_recv, inc_send, inc_recv, out_send, out_recv, rim_sem,
):
    sg = lax.axis_index("segment")
    q = lax.axis_index("seq")
    n_sg = lax.axis_size("segment")
    n_q = lax.axis_size("seq")
    y, x = q // PARTS, q % PARTS
    before, after = (q + n_q - 1) % n_q, (q + 1) % n_q
    sg_to, sg_from = (sg + n_sg - 1) % n_sg, (sg + 1) % n_sg

    def row_mate(k):
        return y * PARTS + (x + k) % PARTS

    def col_mate(k):
        return ((y + k) % ROWS) * PARTS + x

    loads = []
    for c in range(PARTS):
        cols = pl.ds(c * WIDTH, WIDTH)
        loads.append((
            pltpu.make_async_copy(feat.at[0, :, cols], feat_v.at[c], load_sem.at[0, c]),
            pltpu.make_async_copy(cot.at[0, :, cols], cot_v.at[c], load_sem.at[1, c]),
        ))
    pars = [
        pltpu.make_async_copy(taps, tap_t, par_sem.at[0]),
        pltpu.make_async_copy(res.at[0], res_v, par_sem.at[1]),
        pltpu.make_async_copy(rates.at[0], rates_v, par_sem.at[2]),
    ]
    rim = [
        pltpu.make_async_copy(feat.at[0, pl.ds(0, 16), :], feat_e.at[0], rim_sem.at[0]),
        pltpu.make_async_copy(feat.at[0, pl.ds(TOK - 16, 16), :], feat_e.at[1], rim_sem.at[1]),
        pltpu.make_async_copy(cot.at[0, pl.ds(0, 16), :], cot_e, rim_sem.at[2]),
    ]
    for copy in rim:
        copy.start()
    for copy in loads[0]:
        copy.start()
    for copy in pars:
        copy.start()
    for pair in loads[1:]:
        for copy in pair:
            copy.start()

    barrier = pltpu.get_barrier_semaphore()

    def greet(**where):
        pl.semaphore_signal(barrier, inc=1, device_id=where, device_id_type=MESH)

    for k in range(1, PARTS):
        greet(seq=row_mate(k))
    for k in range(1, ROWS):
        greet(seq=col_mate(k))
    greet(seq=before)
    greet(seq=after)
    greet(segment=sg_to)
    greet(segment=sg_from)

    ends = []
    run = jnp.int32(0)
    for i in range(DOCS):
        run = run + lens[0, i]
        ends.append(jnp.full((GROUP, LANES), run, jnp.int32))

    def doc_at(position):
        spot = jnp.full((GROUP, LANES), position, jnp.int32)
        count = total_of([jnp.where(end <= spot, 1, 0) for end in ends])
        return jnp.where(spot < 0, -1, count)

    def same(a, b):
        return jnp.where(a == b, 1.0, 0.0).astype(F32)

    first = q * TOK
    doc_tail = doc_at(first + TOK - 1)
    doc_head = doc_at(first + HALO)
    doc_in = doc_at(first - 1)
    doc_out = doc_at(first + ES)

    def mask_step(e, carry):
        d1, d2 = carry
        d0 = doc_at(first + e)
        put(k1, e, same(d0, d1))
        put(k2, e, same(d0, d2))
        put(mt, e, same(d0, doc_tail))
        put(mh, e, same(d0, doc_head))
        put(mi, e, same(d0, doc_in))
        put(mo, e, same(d0, doc_out))
        return d0, d1

    lax.fori_loop(0, XS, mask_step, (doc_at(first - 1), doc_at(first - 2)))

    def relay(c):
        for which, (far, near_v) in enumerate(((feat, feat_v), (cot, cot_v))):
            pltpu.make_async_copy(
                far.at[0, :, pl.ds(0, WIDTH)], near_v.at[c], load_sem.at[which, c]
            ).wait()

        def rows(t, _):
            for source, target, shift in ((feat_v, xt, HALO), (cot_v, gt, 0)):
                for g in range(GROUP):
                    value = source[
                        c, pl.ds(pl.multiple_of(t * 16, 16), 16), g * LANES : (g + 1) * LANES
                    ].astype(F32)
                    target[c, pl.ds((shift + t * 16) * GROUP + g, 16, stride=GROUP), :] = value
            return 0

        lax.fori_loop(1, TOK // 16 - 1, rows, 0)
        t = TOK // 16 - 1
        for g in range(GROUP):
            value = cot_v[c, t * 16 : TOK, g * LANES : (g + 1) * LANES].astype(F32)
            gt[c, pl.ds(t * 16 * GROUP + g, 16, stride=GROUP), :] = value

    halo_copies = [
        pltpu.make_async_remote_copy(
            src_ref=ref.at[:, pl.ds(here * GROUP, HALO * GROUP), :],
            dst_ref=ref.at[:, pl.ds(there * GROUP, HALO * GROUP), :],
            send_sem=halo_send.at[n],
            recv_sem=halo_recv.at[n],
            device_id={"seq": to},
            device_id_type=MESH,
        )
        for n, (ref, here, there, to) in enumerate((
            (xt, TOK, 0, after),
            (xt, HALO, TOK + HALO, before),
            (gt, 0, TOK, before),
        ))
    ]

    for copy in rim:
        copy.wait()
    for c in range(PARTS):
        for g in range(GROUP):
            cols = slice(c * WIDTH + g * LANES, c * WIDTH + (g + 1) * LANES)
            spread = pl.ds(HALO * GROUP + g, 16, stride=GROUP)
            xt[c, spread, :] = feat_e[0, :, cols].astype(F32)
            spread = pl.ds((HALO + TOK - 16) * GROUP + g, 16, stride=GROUP)
            xt[c, spread, :] = feat_e[1, :, cols].astype(F32)
            gt[c, pl.ds(g, 16, stride=GROUP), :] = cot_e[:, cols].astype(F32)
    pl.semaphore_wait(barrier, (PARTS - 1) + (ROWS - 1) + 4)
    for copy in halo_copies:
        copy.start()

    for copy in pars:
        copy.wait()
    for c in range(PARTS):
        for g in range(GROUP):
            cols = slice(c * WIDTH + g * LANES, c * WIDTH + (g + 1) * LANES)
            rate = rates_v[:, cols]
            spread = pl.ds(c * STATE + g, POLES, stride=GROUP)
            dec[spread, :] = jnp.exp(-rate)
            near[spread, :] = jnp.exp(-rate * float(TOK - HALO))
            past[spread, :] = jnp.exp(-rate * float(ES))
            grow[spread, :] = jnp.exp(rate)
            dd[spread, :] = jnp.exp(-rate * float(TOK))
            dd4[spread, :] = jnp.exp(-rate * float(TOK * PARTS))
            wts[spread, :] = res_v[:, cols] * jnp.sqrt(2.0 * rate)

    def cells(ref, at, count=CELL):
        return ref.at[pl.ds(pl.multiple_of(at * GROUP, GROUP), count * GROUP), :]

    def cell(c, who, way, pole):
        return ((c * PARTS + who) * 2 + way) * PAIR + pole

    def tail_copy(c, k):
        other = (x + k) % PARTS
        return pltpu.make_async_remote_copy(
            src_ref=cells(tails, cell(c, other, 0, 0)),
            dst_ref=cells(row_in, cell(c, x, 0, 0)),
            send_sem=tail_send.at[c, k],
            recv_sem=tail_recv.at[c, k],
            device_id={"seq": row_mate(k)},
            device_id_type=MESH,
        )

    def col_copy(c, way, k):
        slot = way * REACH + k - 1
        return pltpu.make_async_remote_copy(
            src_ref=cells(sums, (c * 2 + way) * PAIR, PAIR),
            dst_ref=cells(col_in, (c * 2 * REACH + slot) * PAIR, PAIR),
            send_sem=col_send.at[c, slot],
            recv_sem=col_recv.at[c, slot],
            device_id={"seq": col_mate(k if way == 0 else ROWS - k)},
            device_id_type=MESH,
        )

    def inc_copy(c, k):
        other = (x + k) % PARTS
        return pltpu.make_async_remote_copy(
            src_ref=cells(sent, cell(c, other, 0, 0)),
            dst_ref=cells(inc, cell(c, x, 0, 0)),
            send_sem=inc_send.at[c, k],
            recv_sem=inc_recv.at[c, k],
            device_id={"seq": row_mate(k)},
            device_id_type=MESH,
        )

    row_first = y * PARTS * TOK
    row_span = TOK * PARTS

    def row_links():
        fwd = [doc_at(row_first + n * TOK - 1) for n in range(PARTS + 1)]
        bwd = [doc_at(row_first + n * TOK + HALO) for n in range(PARTS + 1)]
        return [[same(docs[n], docs[n + 1]) for n in range(PARTS)] for docs in (fwd, bwd)]

    def col_links():
        gone = [doc_at(row_first - k * row_span - 1) for k in range(REACH)]
        coming = [doc_at(row_first + k * row_span + HALO) for k in range(1, REACH + 1)]
        return [[same(docs[n], docs[n + 1]) for n in range(REACH - 1)] for docs in (gone, coming)]

    for way, links in enumerate(row_links()):
        for n, link in enumerate(links):
            put(row_link, way * PARTS + n, link)
    for way, links in enumerate(col_links()):
        for n, link in enumerate(links):
            put(col_link, way * PARTS + n, link)

    def along_row(c):
        for k in range(1, PARTS):
            tail_copy(c, k).wait_recv()
        for pole in range(PAIR):
            span = tile(dd, c * POLES + x * PAIR + pole)
            for way in range(2):
                order = list(range(PARTS)) if way == 0 else list(range(PARTS - 1, -1, -1))
                state = tile(row_in, cell(c, order[0], way, pole))
                for n in order[1:]:
                    link = tile(row_link, way * PARTS + n)
                    state = tile(row_in, cell(c, n, way, pole)) + link * span * state
                put(sums, (c * 2 + way) * PAIR + pole, state)
        for k in range(1, REACH + 1):
            for way in range(2):
                col_copy(c, way, k).start()

    def entering(c):
        for k in range(1, REACH + 1):
            for way in range(2):
                col_copy(c, way, k).wait_recv()
        for pole in range(PAIR):
            at = c * POLES + x * PAIR + pole
            span, long_span = tile(dd, at), tile(dd4, at)
            for way in range(2):
                slot = (c * 2 + way) * REACH
                state = tile(col_in, (slot + REACH - 1) * PAIR + pole)
                for k in range(REACH - 1, 0, -1):
                    link = tile(col_link, way * PARTS + k - 1)
                    state = tile(col_in, (slot + k - 1) * PAIR + pole) + link * long_span * state
                order = range(PARTS) if way == 0 else range(PARTS - 1, -1, -1)
                for n in order:
                    put(sent, cell(c, n, way, pole), state)
                    link = tile(row_link, way * PARTS + n)
                    state = tile(row_in, cell(c, n, way, pole)) + link * span * state
        for k in range(1, PARTS):
            inc_copy(c, k).start()
        for n in range(CELL):
            put(inc, cell(c, x, 0, n), tile(sent, cell(c, x, 0, n)))

    def xtile(c, slot):
        return xt[c, pl.ds(pl.multiple_of(slot * GROUP, GROUP), GROUP), :]

    def gtile(c, e):
        return gt[c, pl.ds(pl.multiple_of(e * GROUP, GROUP), GROUP), :]

    def first_pass(c, _):
        relay(c)
        tap = [tap_t[n, pl.ds(pl.multiple_of(c * GROUP, GROUP), GROUP), :] for n in range(9)]
        e_at = c * ES

        def stream(e, x1, x2):
            x0 = xtile(c, HALO + e)
            a, b = x1 * tile(k1, e), x2 * tile(k2, e)
            gate, key, value = (
                tap[3 * n] * x0 + tap[3 * n + 1] * a + tap[3 * n + 2] * b for n in range(3)
            )
            grad = gtile(c, e) * gate
            put(kt, e_at + e, key)
            put(vt, e_at + e, value)
            put(gft, e_at + e, grad)
            return x0, key * value, grad

        def streams(i, carry):
            x1, x2 = carry
            for u in range(6):
                x0, _, _ = stream(HALO + i * 6 + u, x1, x2)
                x1, x2 = x0, x1
            return x1, x2

        inner = TOK - HALO
        lax.fori_loop(0, inner // 6, streams, (xtile(c, HALO + 1), xtile(c, HALO)))

        decay = [tile(dec, c * POLES + p) for p in range(POLES)]

        def ends_step(i, carry):
            fwd, bwd = carry
            for u in range(3):
                e = HALO + i * 3 + u
                r = TOK - 1 - (i * 3 + u)
                mixed = tile(kt, e_at + e) * tile(vt, e_at + e) * tile(mt, e)
                grad = tile(gft, e_at + r) * tile(mh, r)
                fwd = tuple(d * s + mixed for d, s in zip(decay, fwd))
                bwd = tuple(d * s + grad for d, s in zip(decay, bwd))
            return fwd, bwd

        zero = tuple(jnp.zeros((GROUP, LANES), F32) for _ in range(POLES))
        fwd, bwd = lax.fori_loop(0, inner // 3, ends_step, (zero, zero))

        @pl.when(c == 0)
        def _():
            for copy in halo_copies:
                copy.wait_recv()

        x0, mixed0, _ = stream(0, xtile(c, 1), xtile(c, 0))
        _, mixed1, _ = stream(1, x0, xtile(c, 1))
        x0, _, grad0 = stream(TOK, xtile(c, TOK + 1), xtile(c, TOK))
        _, _, grad1 = stream(TOK + 1, x0, xtile(c, TOK + 1))
        mixed0, mixed1 = mixed0 * tile(mt, 0), mixed1 * tile(mt, 1)
        grad0, grad1 = grad0 * tile(mh, TOK), grad1 * tile(mh, TOK + 1)
        for p in range(POLES):
            far = tile(near, c * POLES + p)
            at = (c, p // PAIR)
            put(tails, cell(*at, 0, p % PAIR), fwd[p] + far * (decay[p] * mixed0 + mixed1))
            put(tails, cell(*at, 1, p % PAIR), bwd[p] + far * (decay[p] * grad1 + grad0))
        for k in range(1, PARTS):
            tail_copy(c, k).start()
        for n in range(CELL):
            put(row_in, cell(c, x, 0, n), tile(tails, cell(c, x, 0, n)))

        @pl.when(c >= 2)
        def _():
            along_row(c - 2)

        return 0

    lax.fori_loop(0, PARTS, first_pass, 0)

    def own_filters(c, _):
        e_at = c * ES
        decay = [tile(dec, c * POLES + p) for p in range(POLES)]
        weight = [tile(wts, c * POLES + p) for p in range(POLES)]

        def both(i, carry):
            fwd, bwd = carry
            for u in range(5):
                e = i * 5 + u
                r = ES - 1 - e
                mixed = tile(kt, e_at + e) * tile(vt, e_at + e)
                grad = tile(gft, e_at + r)
                keep, back_keep = tile(k1, e), tile(k1, r + 1)
                fwd = tuple((keep * d) * s + mixed for d, s in zip(decay, fwd))
                bwd = tuple((back_keep * d) * s + grad for d, s in zip(decay, bwd))
                put(ft, e_at + e, total_of([w * s for w, s in zip(weight, fwd)]))
                put(mx, e_at + r, total_of([w * s for w, s in zip(weight, bwd)]))
            return fwd, bwd

        zero = tuple(jnp.zeros((GROUP, LANES), F32) for _ in range(POLES))
        lax.fori_loop(0, ES // 5, both, (zero, zero))

        @pl.when(c < 2)
        def _():
            along_row(c + 2)

        @pl.when((c == 1) | (c == 2))
        def _():
            entering(c - 1)

        return 0

    lax.fori_loop(0, PARTS - 1, own_filters, 0)
    entering(2)

    def out_copies(c, half):
        rows = pl.ds(pl.multiple_of(half * HALF, HALF), HALF)
        cols = pl.ds(pl.multiple_of(c * WIDTH, WIDTH), WIDTH)
        part_rows = pl.ds(pl.multiple_of(c * GROUP, GROUP), GROUP)
        scale_rows = pl.ds(pl.multiple_of((half * PARTS + c) * GROUP, GROUP), GROUP)
        return [
            pltpu.make_async_remote_copy(
                src_ref=source,
                dst_ref=target,
                send_sem=out_send.at[n, c * 2 + half],
                recv_sem=out_recv.at[n, c * 2 + half],
                device_id={"segment": sg_to},
                device_id_type=MESH,
            )
            for n, (source, target) in enumerate((
                (qv.at[c, rows, :], out_q.at[rows, cols]),
                (sv.at[scale_rows, :], (out_early, out_late)[half].at[part_rows, :]),
            ))
        ]

    def second_pass(c, _):
        @pl.when(c == PARTS - 2)
        def _():
            own_filters(PARTS - 1, 0)

        for k in range(1, PARTS):
            inc_copy(c, k).wait_recv()

        e_at = c * ES
        decay = [tile(dec, c * POLES + p) for p in range(POLES)]
        growth = [tile(grow, c * POLES + p) for p in range(POLES)]
        tap = [tap_t[n, pl.ds(pl.multiple_of(c * GROUP, GROUP), GROUP), :] for n in range(9)]

        def back_step(e, carry):
            fwd, bwd, t1, t2, t22 = carry
            key, value = tile(kt, e_at + e), tile(vt, e_at + e)
            filtered = tile(ft, e_at + e) + tile(mi, e) * total_of(fwd)
            mixed = tile(mx, e_at + e) + tile(mo, e) * total_of(bwd)
            grads = (gtile(c, e) * filtered, mixed * value, mixed * key)
            terms = [
                tap[lag] * grads[0] + tap[3 + lag] * grads[1] + tap[6 + lag] * grads[2]
                for lag in range(3)
            ]
            result = terms[0] + tile(k1, e + 1) * t1 + tile(k2, e + 2) * t22
            fwd = tuple(s * d for s, d in zip(fwd, growth))
            bwd = tuple(s * d for s, d in zip(bwd, decay))
            return result, (fwd, bwd, terms[1], terms[2], t2)

        nothing = jnp.zeros((GROUP, LANES), F32)
        fwd, bwd = [], []
        for p in range(POLES):
            weight = tile(wts, c * POLES + p)
            fwd.append(
                weight * tile(past, c * POLES + p) * tile(inc, cell(c, p // PAIR, 0, p % PAIR))
            )
            bwd.append(weight * decay[p] * tile(inc, cell(c, p // PAIR, 1, p % PAIR)))
        carry = (tuple(fwd), tuple(bwd), nothing, nothing, nothing)
        for e in (TOK + 1, TOK):
            _, carry = back_step(e, carry)

        def piece(n, carry):
            half = 1 - n
            last = half * HALF + HALF - 1

            def backward(i, inner):
                carry, most = inner
                for u in range(4):
                    e = last - (i * 4 + u)
                    result, carry = back_step(e, carry)
                    put(ot, e, result)
                    most = jnp.maximum(most, jnp.abs(result))
                return carry, most

            carry, most = lax.fori_loop(0, HALF // 4, backward, (carry, nothing))
            most = jnp.maximum(most, 1e-30)
            put(sv, half * PARTS + c, most * (1.0 / TOP))
            iv[...] = TOP / most

            def coded(i, _):
                t = half * (HALF // 16) + i
                for g in range(GROUP):
                    value = ot[pl.ds(t * 16 * GROUP + g, 16, stride=GROUP), :] * iv[g : g + 1, :]
                    qv[c, pl.ds(pl.multiple_of(t * 16, 16), 16), g * LANES : (g + 1) * LANES] = (
                        jnp.round(value).astype(jnp.int32).astype(jnp.int16)
                    )
                return 0

            lax.fori_loop(0, HALF // 16, coded, 0)
            for copy in out_copies(c, half):
                copy.start()
            return carry

        for n in range(2):
            carry = piece(n, carry)

        @pl.when(c == 0)
        def _():
            entering(PARTS - 1)

        return 0

    lax.fori_loop(0, PARTS, second_pass, 0)

    def finish(c, _):
        for k in range(1, PARTS):
            tail_copy(c, k).wait_send()
            inc_copy(c, k).wait_send()
        for k in range(1, REACH + 1):
            for way in range(2):
                col_copy(c, way, k).wait_send()
        for half in range(2):
            for copy in out_copies(c, half):
                copy.wait()
        return 0

    for copy in halo_copies:
        copy.wait_send()
    lax.fori_loop(0, PARTS, finish, 0)


def shards(features, cotangent, short_taps, residue, decay_rates, lengths):
    tokens, channels = features.shape[1:]
    far = pl.BlockSpec(memory_space=pltpu.HBM)
    bf16 = jnp.bfloat16
    vm = pltpu.VMEM
    dma = pltpu.SemaphoreType.DMA
    whole = lambda rows: vm((rows * GROUP, LANES), F32)
    coded, late, early = pl.pallas_call(
        mixer_kernel,
        out_shape=(
            jax.ShapeDtypeStruct((tokens, channels), jnp.int16),
            jax.ShapeDtypeStruct((PARTS * GROUP, LANES), F32),
            jax.ShapeDtypeStruct((PARTS * GROUP, LANES), F32),
        ),
        in_specs=[far] * 5 + [pl.BlockSpec(memory_space=pltpu.SMEM)],
        out_specs=(far, far, far),
        scratch_shapes=[
            vm((PARTS, TOK, WIDTH), bf16), vm((PARTS, TOK, WIDTH), bf16),
            vm((2, 16, channels), bf16), vm((16, channels), bf16),
            vm((POLES, channels), F32), vm((POLES, channels), F32),
            vm((PARTS, XS * GROUP, LANES), F32), vm((PARTS, ES * GROUP, LANES), F32),
            whole(PARTS * ES), whole(PARTS * ES), whole(PARTS * ES), whole(PARTS * ES),
            whole(PARTS * ES), whole(ES), whole(XS), whole(XS), whole(XS), whole(XS),
            whole(XS), whole(XS),
            vm((9, PARTS * GROUP, LANES), F32), whole(PARTS * POLES), whole(PARTS * POLES),
            whole(PARTS * POLES), whole(PARTS * POLES),
            whole(PARTS * POLES), whole(PARTS * POLES), whole(PARTS * POLES),
            whole(PARTS * 2 * POLES), whole(PARTS * 2 * POLES), whole(PARTS * CELL),
            whole(PARTS * REACH * CELL), whole(PARTS * 2 * POLES), whole(PARTS * 2 * POLES),
            whole(2 * PARTS), whole(2 * PARTS),
            vm((PARTS, TOK, WIDTH), jnp.int16), whole(2 * PARTS), whole(1),
            dma((2, PARTS)), dma((3,)), dma((3,)), dma((3,)),
            dma((PARTS, PARTS)), dma((PARTS, PARTS)),
            dma((PARTS, 2 * REACH)), dma((PARTS, 2 * REACH)),
            dma((PARTS, PARTS)), dma((PARTS, PARTS)), dma((2, 2 * PARTS)), dma((2, 2 * PARTS)),
            dma((3,)),
        ],
        compiler_params=pltpu.CompilerParams(
            collective_id=0, has_side_effects=True, vmem_limit_bytes=60 * 1024 * 1024
        ),
        cost_estimate=pl.CostEstimate(
            flops=160 * tokens * channels, bytes_accessed=8 * tokens * channels, transcendentals=0
        ),
    )(features, cotangent, short_taps.reshape(9, channels // LANES, LANES), residue, decay_rates, lengths)
    first_half = (jnp.arange(tokens) < HALF)[:, None]
    scale = jnp.where(first_half, early.reshape(1, channels), late.reshape(1, channels))
    return (coded.astype(F32) * scale)[None]


def solution(mesh):
    in_specs = (
        P("segment", "seq", None),
        P("segment", "seq", None),
        P("segment", None, None, None),
        P("segment", None, None),
        P("segment", None, None),
        P("segment", None),
    )
    out_specs = P("segment", "seq", None)
    return jax.shard_map(shards, mesh=mesh, in_specs=in_specs, out_specs=out_specs, check_vma=False)
```

time: 60.3 us -> 48 us (0.80)
  the two profiles are of different devices: /device:TPU:4 before, /device:TPU:8 now
where the time goes in v2:
time: 48 us; the launch traced here: 47.8 us
  Pallas kernels  44.8 us (93%)
  other arithmetic  3 us (6%)
    pallas_call x1, Pallas kernels, shards(): pl.pallas_call(mixer_kernel, out_shape=(jax.ShapeDtypeStruct((tokens, cha...  44.8 us
    broadcast_in_dim x1, other arithmetic, shards(): return (coded.astype(F32) * scale)[None]  2.99 us

profile of v2, /device:TPU:8, one launch (start us, length us, event | category | flops | bytes accessed | tf_op | source)
XLA Modules:
  0.0 47.8 jit_solution(15436905183434467047)
XLA Ops:
  0.0 44.8 %shard_map.64 = (s16[128,4096]{1,0:T(8,128)(2,1)}, f32[32,128]{1,0:T(8,128)}, f32[32,128]{1,0:T(8,128)}) custom-call(bf16[1,128,4096]{2,1,0:T(8,128)(2,1)} %feat.1, bf16[1,128,4096]{2,1,0:T(8,128)(2,1)} %cot.1, f32[9,32,128]{2,1,0:T(8,128)} %bitcast.5, f32[1,8,4096]{2,1,0:T(8,128)} %res.1, f32[1,8,4096]{2,1,0:T(8,128)} %rates.1, s32[1,8]{1,0:T(1,128)} %lens.1), custom_call_target="tpu_custom_call" | custom-call | flops 83886080 | bytes 4194304 | tf_op jit(solution)/shard_map/pallas_call | solution.py:547
  44.8 3.0 %multiply_bitcast_fusion = f32[1,128,4096]{2,1,0:T(8,128)} fusion(s16[128,4096]{1,0:T(8,128)(2,1)} %get-tuple-element.8, f32[4096]{0:T(1024)} %bitcast.6, f32[4096]{0:T(1024)} %bitcast.7, pred[128]{0:T(512)(128)(4,1)S(1)} %iota_compare_fusion), kind=kLoop, calls=%fused_computation | loop fusion | flops 1572864 | bytes 3178624 | tf_op jit(solution)/shard_map/broadcast_in_dim | solution.py:586
  (1 shorter events, 0.0 us)

commit v3 on v2

--- a/solution.py
+++ b/solution.py
@@ -24,6 +24,8 @@
 PAIR = POLES // PARTS
 CELL = 2 * PAIR
 TOP = 32767.0
+LENT = PARTS - 1
+OWN = LENT * WIDTH
 
 
 def tile(ref, i):
@@ -45,12 +47,12 @@
 
 def mixer_kernel(
     feat, cot, taps, res, rates, lens, out_q, out_late, out_early,
-    feat_v, cot_v, feat_e, cot_e, res_v, rates_v,
+    feat_v, cot_v, feat_e, cot_e, rim_lent, res_v, rates_v,
     xt, gt, kt, vt, gft, ft, mx, ot, k1, k2, mt, mh, mi, mo,
     tap_t, dec, wts, near, past, grow, dd, dd4,
-    tails, row_in, sums, col_in, sent, inc, row_link, col_link, qv, sv, iv,
+    tails, row_in, sums, col_in, sent, inc, row_link, col_link, ends_own, ends_lent, qv, sv, iv,
     load_sem, par_sem, halo_send, halo_recv, tail_send, tail_recv,
-    col_send, col_recv, inc_send, inc_recv, out_send, out_recv, rim_sem,
+    col_send, col_recv, inc_send, inc_recv, out_send, out_recv, rim_sem, lend_send, lend_recv, kept_sem, ready,
 ):
     sg = lax.axis_index("segment")
     q = lax.axis_index("seq")
@@ -67,16 +69,24 @@
         return ((y + k) % ROWS) * PARTS + x
 
     loads = []
-    for c in range(PARTS):
+    for c in range(LENT):
         cols = pl.ds(c * WIDTH, WIDTH)
         loads.append((
             pltpu.make_async_copy(feat.at[0, :, cols], feat_v.at[c], load_sem.at[0, c]),
             pltpu.make_async_copy(cot.at[0, :, cols], cot_v.at[c], load_sem.at[1, c]),
         ))
     pars = [
-        pltpu.make_async_copy(taps, tap_t, par_sem.at[0]),
-        pltpu.make_async_copy(res.at[0], res_v, par_sem.at[1]),
-        pltpu.make_async_copy(rates.at[0], rates_v, par_sem.at[2]),
+        pltpu.make_async_copy(
+            taps.at[:, pl.ds(0, LENT * GROUP), :],
+            tap_t.at[:, pl.ds(0, LENT * GROUP), :],
+            par_sem.at[0],
+        ),
+        pltpu.make_async_copy(
+            res.at[0, :, pl.ds(0, OWN)], res_v.at[:, pl.ds(0, OWN)], par_sem.at[1]
+        ),
+        pltpu.make_async_copy(
+            rates.at[0, :, pl.ds(0, OWN)], rates_v.at[:, pl.ds(0, OWN)], par_sem.at[2]
+        ),
     ]
     rim = [
         pltpu.make_async_copy(feat.at[0, pl.ds(0, 16), :], feat_e.at[0], rim_sem.at[0]),
@@ -104,82 +114,154 @@
         greet(seq=col_mate(k))
     greet(seq=before)
     greet(seq=after)
-    greet(segment=sg_to)
-    greet(segment=sg_from)
-
-    ends = []
+    last_sg = n_sg - 1
+    three = (q, before, after)
+
+    @pl.when(sg != last_sg)
+    def _():
+        for near_q in three:
+            greet(segment=sg_from, seq=near_q)
+
+    @pl.when(sg == 0)
+    def _():
+        for near_q in three:
+            greet(segment=sg_to, seq=near_q)
+
+
     run = jnp.int32(0)
     for i in range(DOCS):
         run = run + lens[0, i]
-        ends.append(jnp.full((GROUP, LANES), run, jnp.int32))
-
-    def doc_at(position):
-        spot = jnp.full((GROUP, LANES), position, jnp.int32)
-        count = total_of([jnp.where(end <= spot, 1, 0) for end in ends])
-        return jnp.where(spot < 0, -1, count)
+        ends_own[i * GROUP : (i + 1) * GROUP, :] = jnp.full((GROUP, LANES), run, jnp.int32)
+
+    def doc_finder(ends_ref):
+        ends = [ends_ref[i * GROUP : (i + 1) * GROUP, :] for i in range(DOCS)]
+
+        def doc_at(position):
+            spot = jnp.full((GROUP, LANES), position, jnp.int32)
+            count = total_of([jnp.where(end <= spot, 1, 0) for end in ends])
+            return jnp.where(spot < 0, -1, count)
+
+        return doc_at
 
     def same(a, b):
         return jnp.where(a == b, 1.0, 0.0).astype(F32)
 
     first = q * TOK
-    doc_tail = doc_at(first + TOK - 1)
-    doc_head = doc_at(first + HALO)
-    doc_in = doc_at(first - 1)
-    doc_out = doc_at(first + ES)
-
-    def mask_step(e, carry):
-        d1, d2 = carry
-        d0 = doc_at(first + e)
-        put(k1, e, same(d0, d1))
-        put(k2, e, same(d0, d2))
-        put(mt, e, same(d0, doc_tail))
-        put(mh, e, same(d0, doc_head))
-        put(mi, e, same(d0, doc_in))
-        put(mo, e, same(d0, doc_out))
-        return d0, d1
-
-    lax.fori_loop(0, XS, mask_step, (doc_at(first - 1), doc_at(first - 2)))
-
-    def relay(c):
-        for which, (far, near_v) in enumerate(((feat, feat_v), (cot, cot_v))):
-            pltpu.make_async_copy(
-                far.at[0, :, pl.ds(0, WIDTH)], near_v.at[c], load_sem.at[which, c]
-            ).wait()
+    row_first = y * PARTS * TOK
+    row_span = TOK * PARTS
+
+    def masks(ends_ref, which):
+        doc_at = doc_finder(ends_ref)
+        doc_tail = doc_at(first + TOK - 1)
+        doc_head = doc_at(first + HALO)
+        doc_in = doc_at(first - 1)
+        doc_out = doc_at(first + ES)
+        at = which * XS
+
+        def mask_step(e, carry):
+            d1, d2 = carry
+            d0 = doc_at(first + e)
+            put(k1, at + e, same(d0, d1))
+            put(k2, at + e, same(d0, d2))
+            put(mt, at + e, same(d0, doc_tail))
+            put(mh, at + e, same(d0, doc_head))
+            put(mi, at + e, same(d0, doc_in))
+            put(mo, at + e, same(d0, doc_out))
+            return d0, d1
+
+        lax.fori_loop(0, XS, mask_step, (doc_at(first - 1), doc_at(first - 2)))
+
+        fwd = [doc_at(row_first + n * TOK - 1) for n in range(PARTS + 1)]
+        bwd = [doc_at(row_first + n * TOK + HALO) for n in range(PARTS + 1)]
+        gone = [doc_at(row_first - k * row_span - 1) for k in range(REACH)]
+        coming = [doc_at(row_first + k * row_span + HALO) for k in range(1, REACH + 1)]
+        for ref, pairs in ((row_link, (fwd, bwd)), (col_link, (gone, coming))):
+            for way, docs in enumerate(pairs):
+                for n in range(len(docs) - 1):
+                    put(ref, (which * 2 + way) * PARTS + n, same(docs[n], docs[n + 1]))
+
+    masks(ends_own, 0)
+
+    def move(source, target, shift, c, t):
+        for g in range(GROUP):
+            value = source[
+                c, pl.ds(pl.multiple_of(t * 16, 16), 16), g * LANES : (g + 1) * LANES
+            ].astype(F32)
+            target[c, pl.ds((shift + t * 16) * GROUP + g, 16, stride=GROUP), :] = value
+
+    def relay(c, lent):
+        if not lent:
+            for which, (far, near_v) in enumerate(((feat, feat_v), (cot, cot_v))):
+                pltpu.make_async_copy(
+                    far.at[0, :, pl.ds(0, WIDTH)], near_v.at[c], load_sem.at[which, c]
+                ).wait()
 
         def rows(t, _):
-            for source, target, shift in ((feat_v, xt, HALO), (cot_v, gt, 0)):
+            move(feat_v, xt, HALO, c, t)
+            move(cot_v, gt, 0, c, t)
+            return 0
+
+        tiles = TOK // 16
+        if lent:
+            lax.fori_loop(0, tiles, rows, 0)
+            for n, (target, slot, row) in enumerate((
+                (xt, 0, 16 - HALO), (xt, TOK + HALO, 0), (gt, TOK, 0)
+            )):
                 for g in range(GROUP):
-                    value = source[
-                        c, pl.ds(pl.multiple_of(t * 16, 16), 16), g * LANES : (g + 1) * LANES
-                    ].astype(F32)
-                    target[c, pl.ds((shift + t * 16) * GROUP + g, 16, stride=GROUP), :] = value
-            return 0
-
-        lax.fori_loop(1, TOK // 16 - 1, rows, 0)
-        t = TOK // 16 - 1
-        for g in range(GROUP):
-            value = cot_v[c, t * 16 : TOK, g * LANES : (g + 1) * LANES].astype(F32)
-            gt[c, pl.ds(t * 16 * GROUP + g, 16, stride=GROUP), :] = value
-
-    halo_copies = [
+                    value = rim_lent[n, :, g * LANES : (g + 1) * LANES].astype(F32)
+                    target[c, pl.ds(slot * GROUP + g, HALO, stride=GROUP), :] = value[
+                        row : row + HALO
+                    ]
+        else:
+            lax.fori_loop(1, tiles - 1, rows, 0)
+            move(cot_v, gt, 0, c, tiles - 1)
+
+    def halo_set(parts, at):
+        return [
+            pltpu.make_async_remote_copy(
+                src_ref=ref.at[parts, pl.ds(here * GROUP, HALO * GROUP), :],
+                dst_ref=ref.at[parts, pl.ds(there * GROUP, HALO * GROUP), :],
+                send_sem=halo_send.at[at + n],
+                recv_sem=halo_recv.at[at + n],
+                device_id={"seq": to},
+                device_id_type=MESH,
+            )
+            for n, (ref, here, there, to) in enumerate((
+                (xt, TOK, 0, after),
+                (xt, HALO, TOK + HALO, before),
+                (gt, 0, TOK, before),
+            ))
+        ]
+
+    halo_copies = halo_set(pl.ds(0, LENT), 0)
+
+    lent_cols = pl.ds(OWN, WIDTH)
+    lent_tiles = pl.ds(LENT * GROUP, GROUP)
+    lend_copies = [
         pltpu.make_async_remote_copy(
-            src_ref=ref.at[:, pl.ds(here * GROUP, HALO * GROUP), :],
-            dst_ref=ref.at[:, pl.ds(there * GROUP, HALO * GROUP), :],
-            send_sem=halo_send.at[n],
-            recv_sem=halo_recv.at[n],
-            device_id={"seq": to},
+            src_ref=source,
+            dst_ref=target,
+            send_sem=lend_send.at[n],
+            recv_sem=lend_recv.at[n],
+            device_id={"segment": sg_to, "seq": to},
             device_id_type=MESH,
         )
-        for n, (ref, here, there, to) in enumerate((
-            (xt, TOK, 0, after),
-            (xt, HALO, TOK + HALO, before),
-            (gt, 0, TOK, before),
+        for n, (source, target, to) in enumerate((
+            (ends_own, ends_lent, q),
+            (taps.at[:, lent_tiles, :], tap_t.at[:, lent_tiles, :], q),
+            (res.at[0, :, lent_cols], res_v.at[:, lent_cols], q),
+            (rates.at[0, :, lent_cols], rates_v.at[:, lent_cols], q),
+            (feat.at[0, pl.ds(TOK - 16, 16), lent_cols], rim_lent.at[0], after),
+            (feat.at[0, pl.ds(0, 16), lent_cols], rim_lent.at[1], before),
+            (cot.at[0, pl.ds(0, 16), lent_cols], rim_lent.at[2], before),
+            (feat.at[0, :, lent_cols], feat_v.at[LENT], q),
+            (cot.at[0, :, lent_cols], cot_v.at[LENT], q),
         ))
     ]
 
     for copy in rim:
         copy.wait()
-    for c in range(PARTS):
+    for c in range(LENT):
         for g in range(GROUP):
             cols = slice(c * WIDTH + g * LANES, c * WIDTH + (g + 1) * LANES)
             spread = pl.ds(HALO * GROUP + g, 16, stride=GROUP)
@@ -187,13 +269,25 @@
             spread = pl.ds((HALO + TOK - 16) * GROUP + g, 16, stride=GROUP)
             xt[c, spread, :] = feat_e[1, :, cols].astype(F32)
             gt[c, pl.ds(g, 16, stride=GROUP), :] = cot_e[:, cols].astype(F32)
-    pl.semaphore_wait(barrier, (PARTS - 1) + (ROWS - 1) + 4)
+    across = len(three) * ((sg + last_sg) // n_sg + sg // last_sg)
+    pl.semaphore_wait(barrier, (PARTS - 1) + (ROWS - 1) + 2 + across)
     for copy in halo_copies:
         copy.start()
 
-    for copy in pars:
-        copy.wait()
-    for c in range(PARTS):
+    @pl.when(sg == last_sg)
+    def _():
+        for near_q in three:
+            pl.semaphore_signal(
+                ready, inc=1, device_id={"segment": sg_from, "seq": near_q}, device_id_type=MESH
+            )
+
+    @pl.when(sg != 0)
+    def _():
+        for copy in lend_copies:
+            copy.start()
+
+
+    def parameters(c):
         for g in range(GROUP):
             cols = slice(c * WIDTH + g * LANES, c * WIDTH + (g + 1) * LANES)
             rate = rates_v[:, cols]
@@ -206,6 +300,11 @@
             dd4[spread, :] = jnp.exp(-rate * float(TOK * PARTS))
             wts[spread, :] = res_v[:, cols] * jnp.sqrt(2.0 * rate)
 
+    for copy in pars:
+        copy.wait()
+    for c in range(LENT):
+        parameters(c)
+
     def cells(ref, at, count=CELL):
         return ref.at[pl.ds(pl.multiple_of(at * GROUP, GROUP), count * GROUP), :]
 
@@ -245,26 +344,6 @@
             device_id_type=MESH,
         )
 
-    row_first = y * PARTS * TOK
-    row_span = TOK * PARTS
-
-    def row_links():
-        fwd = [doc_at(row_first + n * TOK - 1) for n in range(PARTS + 1)]
-        bwd = [doc_at(row_first + n * TOK + HALO) for n in range(PARTS + 1)]
-        return [[same(docs[n], docs[n + 1]) for n in range(PARTS)] for docs in (fwd, bwd)]
-
-    def col_links():
-        gone = [doc_at(row_first - k * row_span - 1) for k in range(REACH)]
-        coming = [doc_at(row_first + k * row_span + HALO) for k in range(1, REACH + 1)]
-        return [[same(docs[n], docs[n + 1]) for n in range(REACH - 1)] for docs in (gone, coming)]
-
-    for way, links in enumerate(row_links()):
-        for n, link in enumerate(links):
-            put(row_link, way * PARTS + n, link)
-    for way, links in enumerate(col_links()):
-        for n, link in enumerate(links):
-            put(col_link, way * PARTS + n, link)
-
     def along_row(c):
         for k in range(1, PARTS):
             tail_copy(c, k).wait_recv()
@@ -274,7 +353,7 @@
                 order = list(range(PARTS)) if way == 0 else list(range(PARTS - 1, -1, -1))
                 state = tile(row_in, cell(c, order[0], way, pole))
                 for n in order[1:]:
-                    link = tile(row_link, way * PARTS + n)
+                    link = tile(row_link, ((c // LENT) * 2 + way) * PARTS + n)
                     state = tile(row_in, cell(c, n, way, pole)) + link * span * state
                 put(sums, (c * 2 + way) * PAIR + pole, state)
         for k in range(1, REACH + 1):
@@ -292,12 +371,12 @@
                 slot = (c * 2 + way) * REACH
                 state = tile(col_in, (slot + REACH - 1) * PAIR + pole)
                 for k in range(REACH - 1, 0, -1):
-                    link = tile(col_link, way * PARTS + k - 1)
+                    link = tile(col_link, ((c // LENT) * 2 + way) * PARTS + k - 1)
                     state = tile(col_in, (slot + k - 1) * PAIR + pole) + link * long_span * state
                 order = range(PARTS) if way == 0 else range(PARTS - 1, -1, -1)
                 for n in order:
                     put(sent, cell(c, n, way, pole), state)
-                    link = tile(row_link, way * PARTS + n)
+                    link = tile(row_link, ((c // LENT) * 2 + way) * PARTS + n)
                     state = tile(row_in, cell(c, n, way, pole)) + link * span * state
         for k in range(1, PARTS):
             inc_copy(c, k).start()
@@ -310,14 +389,15 @@
     def gtile(c, e):
         return gt[c, pl.ds(pl.multiple_of(e * GROUP, GROUP), GROUP), :]
 
-    def first_pass(c, _):
-        relay(c)
+    def first_pass(c, lent):
+        relay(c, lent)
+        m_at = (c // LENT) * XS
         tap = [tap_t[n, pl.ds(pl.multiple_of(c * GROUP, GROUP), GROUP), :] for n in range(9)]
         e_at = c * ES
 
         def stream(e, x1, x2):
             x0 = xtile(c, HALO + e)
-            a, b = x1 * tile(k1, e), x2 * tile(k2, e)
+            a, b = x1 * tile(k1, m_at + e), x2 * tile(k2, m_at + e)
             gate, key, value = (
                 tap[3 * n] * x0 + tap[3 * n + 1] * a + tap[3 * n + 2] * b for n in range(3)
             )
@@ -344,8 +424,8 @@
             for u in range(3):
                 e = HALO + i * 3 + u
                 r = TOK - 1 - (i * 3 + u)
-                mixed = tile(kt, e_at + e) * tile(vt, e_at + e) * tile(mt, e)
-                grad = tile(gft, e_at + r) * tile(mh, r)
+                mixed = tile(kt, e_at + e) * tile(vt, e_at + e) * tile(mt, m_at + e)
+                grad = tile(gft, e_at + r) * tile(mh, m_at + r)
                 fwd = tuple(d * s + mixed for d, s in zip(decay, fwd))
                 bwd = tuple(d * s + grad for d, s in zip(decay, bwd))
             return fwd, bwd
@@ -353,17 +433,20 @@
         zero = tuple(jnp.zeros((GROUP, LANES), F32) for _ in range(POLES))
         fwd, bwd = lax.fori_loop(0, inner // 3, ends_step, (zero, zero))
 
-        @pl.when(c == 0)
-        def _():
-            for copy in halo_copies:
-                copy.wait_recv()
+        if not lent:
+
+            @pl.when(c == 0)
+            def _():
+                for copy in halo_copies:
+                    copy.wait_recv()
 
         x0, mixed0, _ = stream(0, xtile(c, 1), xtile(c, 0))
         _, mixed1, _ = stream(1, x0, xtile(c, 1))
         x0, _, grad0 = stream(TOK, xtile(c, TOK + 1), xtile(c, TOK))
         _, _, grad1 = stream(TOK + 1, x0, xtile(c, TOK + 1))
-        mixed0, mixed1 = mixed0 * tile(mt, 0), mixed1 * tile(mt, 1)
-        grad0, grad1 = grad0 * tile(mh, TOK), grad1 * tile(mh, TOK + 1)
+        mixed0, mixed1 = mixed0 * tile(mt, m_at), mixed1 * tile(mt, m_at + 1)
+        grad0 = grad0 * tile(mh, m_at + TOK)
+        grad1 = grad1 * tile(mh, m_at + TOK + 1)
         for p in range(POLES):
             far = tile(near, c * POLES + p)
             at = (c, p // PAIR)
@@ -374,16 +457,11 @@
         for n in range(CELL):
             put(row_in, cell(c, x, 0, n), tile(tails, cell(c, x, 0, n)))
 
-        @pl.when(c >= 2)
-        def _():
-            along_row(c - 2)
-
         return 0
 
-    lax.fori_loop(0, PARTS, first_pass, 0)
-
-    def own_filters(c, _):
+    def own_filters(c):
         e_at = c * ES
+        m_at = (c // LENT) * XS
         decay = [tile(dec, c * POLES + p) for p in range(POLES)]
         weight = [tile(wts, c * POLES + p) for p in range(POLES)]
 
@@ -394,7 +472,7 @@
                 r = ES - 1 - e
                 mixed = tile(kt, e_at + e) * tile(vt, e_at + e)
                 grad = tile(gft, e_at + r)
-                keep, back_keep = tile(k1, e), tile(k1, r + 1)
+                keep, back_keep = tile(k1, m_at + e), tile(k1, m_at + r + 1)
                 fwd = tuple((keep * d) * s + mixed for d, s in zip(decay, fwd))
                 bwd = tuple((back_keep * d) * s + grad for d, s in zip(decay, bwd))
                 put(ft, e_at + e, total_of([w * s for w, s in zip(weight, fwd)]))
@@ -404,18 +482,30 @@
         zero = tuple(jnp.zeros((GROUP, LANES), F32) for _ in range(POLES))
         lax.fori_loop(0, ES // 5, both, (zero, zero))
 
-        @pl.when(c < 2)
-        def _():
-            along_row(c + 2)
-
-        @pl.when((c == 1) | (c == 2))
-        def _():
-            entering(c - 1)
-
-        return 0
-
-    lax.fori_loop(0, PARTS - 1, own_filters, 0)
-    entering(2)
+    lax.fori_loop(0, LENT, lambda c, _: first_pass(c, False), 0)
+    for copy in lend_copies[:4]:
+        copy.wait_recv()
+    masks(ends_lent, 1)
+    parameters(LENT)
+    along_row(0)
+
+    @pl.when(sg == 0)
+    def _():
+        pl.semaphore_wait(ready, len(three))
+        for copy in lend_copies:
+            copy.start()
+
+    for copy in lend_copies[4:]:
+        copy.wait_recv()
+    first_pass(LENT, True)
+    along_row(1)
+    own_filters(0)
+    along_row(2)
+    own_filters(1)
+    entering(0)
+    along_row(LENT)
+    own_filters(2)
+    entering(1)
 
     def out_copies(c, half):
         rows = pl.ds(pl.multiple_of(half * HALF, HALF), HALF)
@@ -437,15 +527,26 @@
             ))
         ]
 
+    def kept_copies(half):
+        rows = pl.ds(half * HALF, HALF)
+        scale_rows = pl.ds((half * PARTS + LENT) * GROUP, GROUP)
+        return [
+            pltpu.make_async_copy(
+                qv.at[LENT, rows, :], out_q.at[rows, lent_cols], kept_sem.at[0, half]
+            ),
+            pltpu.make_async_copy(
+                sv.at[scale_rows, :],
+                (out_early, out_late)[half].at[lent_tiles, :],
+                kept_sem.at[1, half],
+            ),
+        ]
+
     def second_pass(c, _):
-        @pl.when(c == PARTS - 2)
-        def _():
-            own_filters(PARTS - 1, 0)
-
         for k in range(1, PARTS):
             inc_copy(c, k).wait_recv()
 
         e_at = c * ES
+        m_at = (c // LENT) * XS
         decay = [tile(dec, c * POLES + p) for p in range(POLES)]
         growth = [tile(grow, c * POLES + p) for p in range(POLES)]
         tap = [tap_t[n, pl.ds(pl.multiple_of(c * GROUP, GROUP), GROUP), :] for n in range(9)]
@@ -453,14 +554,14 @@
         def back_step(e, carry):
             fwd, bwd, t1, t2, t22 = carry
             key, value = tile(kt, e_at + e), tile(vt, e_at + e)
-            filtered = tile(ft, e_at + e) + tile(mi, e) * total_of(fwd)
-            mixed = tile(mx, e_at + e) + tile(mo, e) * total_of(bwd)
+            filtered = tile(ft, e_at + e) + tile(mi, m_at + e) * total_of(fwd)
+            mixed = tile(mx, e_at + e) + tile(mo, m_at + e) * total_of(bwd)
             grads = (gtile(c, e) * filtered, mixed * value, mixed * key)
             terms = [
                 tap[lag] * grads[0] + tap[3 + lag] * grads[1] + tap[6 + lag] * grads[2]
                 for lag in range(3)
             ]
-            result = terms[0] + tile(k1, e + 1) * t1 + tile(k2, e + 2) * t22
+            result = terms[0] + tile(k1, m_at + e + 1) * t1 + tile(k2, m_at + e + 2) * t22
             fwd = tuple(s * d for s, d in zip(fwd, growth))
             bwd = tuple(s * d for s, d in zip(bwd, decay))
             return result, (fwd, bwd, terms[1], terms[2], t2)
@@ -505,8 +606,17 @@
                 return 0
 
             lax.fori_loop(0, HALF // 16, coded, 0)
-            for copy in out_copies(c, half):
-                copy.start()
+
+            @pl.when(c < LENT)
+            def _():
+                for copy in out_copies(c, half):
+                    copy.start()
+
+            @pl.when(c == LENT)
+            def _():
+                for copy in kept_copies(half):
+                    copy.start()
+
             return carry
 
         for n in range(2):
@@ -514,7 +624,12 @@
 
         @pl.when(c == 0)
         def _():
-            entering(PARTS - 1)
+            entering(2)
+
+        @pl.when(c == 1)
+        def _():
+            entering(LENT)
+            own_filters(LENT)
 
         return 0
 
@@ -527,14 +642,21 @@
         for k in range(1, REACH + 1):
             for way in range(2):
                 col_copy(c, way, k).wait_send()
+        return 0
+
+    def finish_out(c, _):
         for half in range(2):
             for copy in out_copies(c, half):
                 copy.wait()
         return 0
 
-    for copy in halo_copies:
+    for copy in halo_copies + lend_copies:
         copy.wait_send()
     lax.fori_loop(0, PARTS, finish, 0)
+    lax.fori_loop(0, LENT, finish_out, 0)
+    for half in range(2):
+        for copy in kept_copies(half):
+            copy.wait()
 
 
 def shards(features, cotangent, short_taps, residue, decay_rates, lengths):
@@ -555,24 +677,26 @@
         out_specs=(far, far, far),
         scratch_shapes=[
             vm((PARTS, TOK, WIDTH), bf16), vm((PARTS, TOK, WIDTH), bf16),
-            vm((2, 16, channels), bf16), vm((16, channels), bf16),
+            vm((2, 16, channels), bf16), vm((16, channels), bf16), vm((3, 16, WIDTH), bf16),
             vm((POLES, channels), F32), vm((POLES, channels), F32),
             vm((PARTS, XS * GROUP, LANES), F32), vm((PARTS, ES * GROUP, LANES), F32),
             whole(PARTS * ES), whole(PARTS * ES), whole(PARTS * ES), whole(PARTS * ES),
-            whole(PARTS * ES), whole(ES), whole(XS), whole(XS), whole(XS), whole(XS),
-            whole(XS), whole(XS),
+            whole(PARTS * ES), whole(ES), whole(2 * XS), whole(2 * XS), whole(2 * XS),
+            whole(2 * XS), whole(2 * XS), whole(2 * XS),
             vm((9, PARTS * GROUP, LANES), F32), whole(PARTS * POLES), whole(PARTS * POLES),
             whole(PARTS * POLES), whole(PARTS * POLES),
             whole(PARTS * POLES), whole(PARTS * POLES), whole(PARTS * POLES),
             whole(PARTS * 2 * POLES), whole(PARTS * 2 * POLES), whole(PARTS * CELL),
             whole(PARTS * REACH * CELL), whole(PARTS * 2 * POLES), whole(PARTS * 2 * POLES),
-            whole(2 * PARTS), whole(2 * PARTS),
+            whole(4 * PARTS), whole(4 * PARTS),
+            vm((DOCS * GROUP, LANES), jnp.int32), vm((DOCS * GROUP, LANES), jnp.int32),
             vm((PARTS, TOK, WIDTH), jnp.int16), whole(2 * PARTS), whole(1),
             dma((2, PARTS)), dma((3,)), dma((3,)), dma((3,)),
             dma((PARTS, PARTS)), dma((PARTS, PARTS)),
             dma((PARTS, 2 * REACH)), dma((PARTS, 2 * REACH)),
             dma((PARTS, PARTS)), dma((PARTS, PARTS)), dma((2, 2 * PARTS)), dma((2, 2 * PARTS)),
-            dma((3,)),
+            dma((3,)), dma((9,)), dma((9,)), dma((2, 2)),
+            pltpu.SemaphoreType.REGULAR,
         ],
         compiler_params=pltpu.CompilerParams(
             collective_id=0, has_side_effects=True, vmem_limit_bytes=60 * 1024 * 1024

time: 48 us -> 45.5 us (0.948)
  the two profiles are of different devices: /device:TPU:8 before, /device:TPU:193 now
where the time goes in v3:
time: 45.5 us; the launch traced here: 45.4 us
  Pallas kernels  42.4 us (93%)
  other arithmetic  3 us (7%)
    pallas_call x1, Pallas kernels, shards(): pl.pallas_call(mixer_kernel, out_shape=(jax.ShapeDtypeStruct((tokens, cha...  42.4 us
    broadcast_in_dim x1, other arithmetic, shards(): return (coded.astype(F32) * scale)[None]  2.99 us

profile of v3, /device:TPU:193, one launch (start us, length us, event | category | flops | bytes accessed | tf_op | source)
XLA Modules:
  0.0 45.4 jit_solution(2933016994875503790)
XLA Ops:
  0.0 42.4 %shard_map.64 = (s16[128,4096]{1,0:T(8,128)(2,1)}, f32[32,128]{1,0:T(8,128)}, f32[32,128]{1,0:T(8,128)}) custom-call(bf16[1,128,4096]{2,1,0:T(8,128)(2,1)} %feat.1, bf16[1,128,4096]{2,1,0:T(8,128)(2,1)} %cot.1, f32[9,32,128]{2,1,0:T(8,128)} %bitcast.5, f32[1,8,4096]{2,1,0:T(8,128)} %res.1, f32[1,8,4096]{2,1,0:T(8,128)} %rates.1, s32[1,8]{1,0:T(1,128)} %lens.1), custom_call_target="tpu_custom_call" | custom-call | flops 83886080 | bytes 4194304 | tf_op jit(solution)/shard_map/pallas_call | solution.py:669
  42.4 3.0 %multiply_bitcast_fusion = f32[1,128,4096]{2,1,0:T(8,128)} fusion(s16[128,4096]{1,0:T(8,128)(2,1)} %get-tuple-element.8, f32[4096]{0:T(1024)} %bitcast.6, f32[4096]{0:T(1024)} %bitcast.7, pred[128]{0:T(512)(128)(4,1)S(1)} %iota_compare_fusion), kind=kLoop, calls=%fused_computation | loop fusion | flops 1572864 | bytes 3178624 | tf_op jit(solution)/shard_map/broadcast_in_dim | solution.py:710
  (1 shorter events, 0.0 us)

commit v4 on v3

--- a/solution.py
+++ b/solution.py
@@ -67,6 +67,31 @@
 
     def col_mate(k):
         return ((y + k) % ROWS) * PARTS + x
+
+    barrier = pltpu.get_barrier_semaphore()
+
+    def greet(**where):
+        pl.semaphore_signal(barrier, inc=1, device_id=where, device_id_type=MESH)
+
+    for k in range(1, PARTS):
+        greet(seq=row_mate(k))
+    for k in range(1, ROWS):
+        greet(seq=col_mate(k))
+    greet(seq=before)
+    greet(seq=after)
+    last_sg = n_sg - 1
+    three = (q, before, after)
+
+    @pl.when(sg != last_sg)
+    def _():
+        for near_q in three:
+            greet(segment=sg_from, seq=near_q)
+
+    @pl.when(sg == 0)
+    def _():
+        for near_q in three:
+            greet(segment=sg_to, seq=near_q)
+
 
     loads = []
     for c in range(LENT):
@@ -103,31 +128,6 @@
         for copy in pair:
             copy.start()
 
-    barrier = pltpu.get_barrier_semaphore()
-
-    def greet(**where):
-        pl.semaphore_signal(barrier, inc=1, device_id=where, device_id_type=MESH)
-
-    for k in range(1, PARTS):
-        greet(seq=row_mate(k))
-    for k in range(1, ROWS):
-        greet(seq=col_mate(k))
-    greet(seq=before)
-    greet(seq=after)
-    last_sg = n_sg - 1
-    three = (q, before, after)
-
-    @pl.when(sg != last_sg)
-    def _():
-        for near_q in three:
-            greet(segment=sg_from, seq=near_q)
-
-    @pl.when(sg == 0)
-    def _():
-        for near_q in three:
-            greet(segment=sg_to, seq=near_q)
-
-
     run = jnp.int32(0)
     for i in range(DOCS):
         run = run + lens[0, i]
@@ -180,7 +180,6 @@
                 for n in range(len(docs) - 1):
                     put(ref, (which * 2 + way) * PARTS + n, same(docs[n], docs[n + 1]))
 
-    masks(ends_own, 0)
 
     def move(source, target, shift, c, t):
         for g in range(GROUP):
@@ -300,6 +299,7 @@
             dd4[spread, :] = jnp.exp(-rate * float(TOK * PARTS))
             wts[spread, :] = res_v[:, cols] * jnp.sqrt(2.0 * rate)
 
+    masks(ends_own, 0)
     for copy in pars:
         copy.wait()
     for c in range(LENT):

time: 45.5 us -> 45.1 us (level)
  Pallas kernels: 42.4 us -> 41.9 us
where the time goes in v4:
time: 45.1 us; the launch traced here: 44.9 us
  Pallas kernels  41.9 us (93%)
  other arithmetic  3 us (7%)
    pallas_call x1, Pallas kernels, shards(): pl.pallas_call(mixer_kernel, out_shape=(jax.ShapeDtypeStruct((tokens, cha...  41.9 us
    broadcast_in_dim x1, other arithmetic, shards(): return (coded.astype(F32) * scale)[None]  2.99 us

profile of v4, /device:TPU:193, one launch (start us, length us, event | category | flops | bytes accessed | tf_op | source)
XLA Modules:
  0.0 44.9 jit_solution(1684249446861379279)
XLA Ops:
  0.0 41.9 %shard_map.64 = (s16[128,4096]{1,0:T(8,128)(2,1)}, f32[32,128]{1,0:T(8,128)}, f32[32,128]{1,0:T(8,128)}) custom-call(bf16[1,128,4096]{2,1,0:T(8,128)(2,1)} %feat.1, bf16[1,128,4096]{2,1,0:T(8,128)(2,1)} %cot.1, f32[9,32,128]{2,1,0:T(8,128)} %bitcast.5, f32[1,8,4096]{2,1,0:T(8,128)} %res.1, f32[1,8,4096]{2,1,0:T(8,128)} %rates.1, s32[1,8]{1,0:T(1,128)} %lens.1), custom_call_target="tpu_custom_call" | custom-call | flops 83886080 | bytes 4194304 | tf_op jit(solution)/shard_map/pallas_call | solution.py:669
  42.0 3.0 %multiply_bitcast_fusion = f32[1,128,4096]{2,1,0:T(8,128)} fusion(s16[128,4096]{1,0:T(8,128)(2,1)} %get-tuple-element.8, f32[4096]{0:T(1024)} %bitcast.6, f32[4096]{0:T(1024)} %bitcast.7, pred[128]{0:T(512)(128)(4,1)S(1)} %iota_compare_fusion), kind=kLoop, calls=%fused_computation | loop fusion | flops 1572864 | bytes 3178624 | tf_op jit(solution)/shard_map/broadcast_in_dim | solution.py:710
  (1 shorter events, 0.0 us)
